TPU v7x, 512 devices: a whole 4x8x8 slice. The times are simulated.
512 devices in a mesh: ifg: 32 (over x, z_hi, core), band: 16 (over z_lo, y).
Axes of the slice: x: 4, y: 8, z: 8 (z_hi: 4, z_lo: 2; z = z_hi * 2 + z_lo), core: 2. Of those that a mesh axis runs over, the one named last changes fastest.
Arguments:
- unwrapped: float32 [1536, 96, 1536], P('ifg', 'band'), may hold values from -6 to 6
- component_mask: int32 [1536, 96, 1536], P('ifg', 'band'), may hold values 0 or 1
- date_pairs: int32 [1536, 2], replicated, may hold values from 0 to 299, as said below
Outputs:
- series: float32 [300, 96, 1536], P(None, 'band', 'ifg')
- corrected: float32 [300, 96, 1536], P(None, 'band', 'ifg')
Inputs may be any that keep to these rules, and one draw needn't show every extreme that they name: `date_pairs`: in each row the first date is earlier than the second and at most 40 dates before it.
All inputs are finite; a program needn't handle non-finite values. No bound on the sum of `component_mask` on one device may be relied on, other than what follows from the above.
Results may differ from a plain program's by a relative error of at most 0.00007.
Values sent between devices are 32-bit elements; how exact they have to be, the bound alone decides.
No kernel may reach another device: no remote copies, remote signals or barrier semaphores. Data moves between devices by JAX's collectives and lax.ppermute only.
A program may use at most 64 MiB of HBM per device.

v0:
```python
import jax
import jax.numpy as jnp
from jax import lax
from jax.sharding import PartitionSpec as P

DATES = 300
TIME_SIGMA = 6
RIM_WIDTH = 4


def extended(shard, sides, width):
    for axis, dim in sides:
        count, length = (lax.axis_size(axis), shard.shape[dim])
        up = [(i, (i + 1) % count) for i in range(count - 1)]
        down = [(j, i) for i, j in up]
        last = lax.slice_in_dim(shard, length - width, length, axis=dim)
        leading = lax.slice_in_dim(shard, 0, width, axis=dim)
        before = lax.ppermute(last, axis, up)
        after = lax.ppermute(leading, axis, down)
        shard = jnp.concatenate([before, shard, after], axis=dim)
    return shard


def pseudo_inverse(date_pairs, num_dates):
    calendar = jnp.arange(num_dates, dtype=jnp.int32)
    design = (date_pairs[:, 1:2] == calendar[None, :]).astype(jnp.float32) - (
        date_pairs[:, 0:1] == calendar[None, :]
    ).astype(jnp.float32)
    normal = jnp.dot(design.T, design, precision=lax.Precision.HIGHEST) + jnp.eye(
        num_dates, dtype=jnp.float32
    )
    factor = jnp.linalg.cholesky(normal)
    return jax.scipy.linalg.cho_solve((factor, True), design.T)


def temporal_highpass(num_dates, sigma):
    offsets = jnp.arange(num_dates, dtype=jnp.int32).astype(jnp.float32)
    spread = offsets[:, None] - offsets[None, :]
    weights = jnp.exp(-spread * spread / (2.0 * sigma * sigma))
    return jnp.eye(num_dates, dtype=jnp.float32) - weights / jnp.sum(weights, axis=1, keepdims=True)


def spatial_taps(width):
    offsets = jnp.arange(-width, width + 1, dtype=jnp.int32).astype(jnp.float32)
    sigma = width / 2.0
    return jnp.exp(-offsets * offsets / (2.0 * sigma * sigma))


def edge_weights(start, count, total, width):
    taps = spatial_taps(width)
    places = (
        start
        + jnp.arange(count, dtype=jnp.int32)[:, None]
        + jnp.arange(-width, width + 1, dtype=jnp.int32)[None, :]
    )
    inside = ((places >= 0) & (places < total)).astype(jnp.float32)
    return jnp.sum(inside * taps[None, :], axis=1)


def along_rows(padded, taps, count):
    result = taps[0] * padded[:, 0:count, :]
    for offset in range(1, 2 * RIM_WIDTH + 1):
        result = result + taps[offset] * padded[:, offset : offset + count, :]
    return result


def along_columns(padded, taps, count):
    result = taps[0] * padded[:, :, 0:count]
    for offset in range(1, 2 * RIM_WIDTH + 1):
        result = result + taps[offset] * padded[:, :, offset : offset + count]
    return result


def body(unwrapped, component_mask, date_pairs):
    rows = unwrapped.shape[1]
    inverse = pseudo_inverse(date_pairs, DATES)
    highpass = temporal_highpass(DATES, TIME_SIGMA)
    masked = unwrapped * component_mask.astype(jnp.float32)
    result = jnp.einsum(
        "tk,krc->trc",
        inverse,
        lax.all_to_all(masked, "ifg", split_axis=2, concat_axis=0, tiled=True),
        precision=lax.Precision.HIGHEST,
    )
    varying = jnp.einsum("st,trc->src", highpass, result, precision=lax.Precision.HIGHEST)
    columns = result.shape[2]
    taps = spatial_taps(RIM_WIDTH)
    row_start = lax.axis_index("band") * rows
    column_start = lax.axis_index("ifg") * columns
    row_norm = edge_weights(row_start, rows, rows * lax.axis_size("band"), RIM_WIDTH)
    column_norm = edge_weights(column_start, columns, columns * lax.axis_size("ifg"), RIM_WIDTH)
    padded = extended(varying, (("band", 1),), RIM_WIDTH)
    rowpass = along_rows(padded, taps, rows) / row_norm[None, :, None]
    widened = extended(rowpass, (("ifg", 2),), RIM_WIDTH)
    atmosphere = along_columns(widened, taps, columns) / column_norm[None, None, :]
    return (result, result - atmosphere)


def solution(mesh):
    placed = (P("ifg", "band", None), P("ifg", "band", None), P())
    return jax.shard_map(
        body,
        mesh=mesh,
        in_specs=placed,
        out_specs=(P(None, "band", "ifg"), P(None, "band", "ifg")),
        check_vma=False,
    )
```

profile of v0, /device:TPU:66, one launch (start us, length us, event | category | flops | bytes accessed | tf_op | source)
XLA Modules:
  0.0 201.2 jit_solution(11697002000149208299)
XLA Ops:
  0.6 2.3 %convert_multiply_fusion = f32[48,6,1536]{2,0,1:T(8,128)S(1)} fusion(f32[48,6,1536]{2,0,1:T(8,128)} %param.3, s32[48,6,1536]{2,0,1:T(8,128)} %param.4), kind=kLoop, calls=%fused_computation.22 | loop fusion | flops 884736 | bytes 5308416 | tf_op jit(solution)/shard_map/mul | solution.py:78
  2.9 4.0 %copy.16 = f32[48,6,1536]{0,1,2:T(8,128)} copy(f32[48,6,1536]{2,0,1:T(8,128)S(1)} %convert_multiply_fusion) | data formatting | bytes 3538944 | tf_op jit(solution)/shard_map/mul | solution.py:78
  7.0 7.2 %reshape.106 = f32[32,1,13824]{2,1,0:T(1,128)} reshape(f32[1536,6,48]{2,1,0:T(8,128)} %bitcast.74) | data formatting | bytes 3538944
  14.2 12.9 %all-to-all-start = ((f32[32,1,13824]{2,1,0:T(1,128)}), f32[32,1,13824]{2,1,0:T(1,128)S(1)}, u32[]{:S(2)}, u32[]{:S(2)}) async-start(f32[32,1,13824]{2,1,0:T(1,128)} %reshape.106), calls=%async_computation | async-start | bytes 3538944 | tf_op jit(solution)/shard_map/all_to_all | solution.py:82
  27.2 5.4 %fusion = f32[300,300]{1,0:T(8,128)S(1)} fusion(s32[1536]{0:T(1024)S(1)} %get-tuple-element.11, s32[1536]{0:T(1024)S(1)} %get-tuple-element.10), kind=kOutput, calls=%fused_computation.6 | convolution fusion | flops 1661184000 | bytes 372288 | tf_op jit(solution)/shard_map/dot_general | solution.py:29
  32.9 11.7 %cholesky.78 = f32[128,128]{1,0:T(8,128)S(1)} custom-call(f32[128,128]{1,0:T(8,128)S(1)} %cholesky.198), custom_call_target="Cholesky" | custom-call | tf_op jit(solution)/shard_map/jit(cholesky)/cholesky | solution.py:32
  44.7 9.8 %custom-call.26 = f32[1,128,128]{1,2,0:T(8,128)S(1)} custom-call(f32[1,128,128]{2,1,0:T(8,128)S(1)} %get-tuple-element.30), custom_call_target="InvertDiagBlocksLowerTriangular" | custom-call | tf_op jit(solution)/shard_map/jit(cholesky)/cholesky | solution.py:32
  55.0 11.9 %cholesky.164 = f32[128,128]{1,0:T(8,128)S(1)} custom-call(f32[128,128]{1,0:T(8,128)S(1)} %cholesky.202), custom_call_target="Cholesky" | custom-call | tf_op jit(solution)/shard_map/jit(cholesky)/cholesky | solution.py:32
  67.0 9.8 %custom-call.27 = f32[1,128,128]{1,2,0:T(8,128)S(1)} custom-call(f32[1,128,128]{2,1,0:T(8,128)S(1)} %get-tuple-element.27), custom_call_target="InvertDiagBlocksLowerTriangular" | custom-call | tf_op jit(solution)/shard_map/jit(cholesky)/cholesky | solution.py:32
  77.2 4.0 %cholesky.186 = f32[44,44]{1,0:T(8,128)S(1)} custom-call(f32[44,44]{1,0:T(8,128)S(1)} %convolution_subtract_fusion.5), custom_call_target="Cholesky" | custom-call | tf_op jit(solution)/shard_map/jit(cholesky)/cholesky | solution.py:32
  84.7 4.1 %while.1 = (s32[]{:T(128)}, f32[300,300]{1,0:T(8,128)S(1)}, s32[2,2]{1,0:T(2,128)S(1)}, f32[2,128,128]{2,1,0:T(8,128)S(1)}, s32[]{:T(128)}) while((s32[]{:T(128)}, f32[300,300]{1,0:T(8,128)S(1)}, s32[2,2]{1,0:T(2,128)S(1)}, f32[2,128,128]{2,1,0:T(8,128)S(1)}, s32[]{:T(128)}) %tuple.40), condition=%wide.while_cond, body=%wide.while_body.sunk | while | flops 2 | bytes 131189 | solution.py:33
  85.3 1.4 bitcast_dynamic-update-slice_fusion.2
  87.4 1.4 bitcast_dynamic-update-slice_fusion.2
  88.9 29.9 %custom-call.28 = f32[3,128,128]{1,2,0:T(8,128)S(1)} custom-call(f32[3,128,128]{2,1,0:T(8,128)S(1)} %pad_maximum_fusion.4), custom_call_target="InvertDiagBlocksLowerTriangular" | custom-call | tf_op jit(solution)/shard_map/jit(_cho_solve)/triangular_solve | solution.py:33
  118.9 0.9 fusion.27
  122.5 1.0 convolution_subtract_fusion.3
  126.9 1.7 fusion.88
  129.2 4.9 %reduce.22 = f32[32,13824]{1,0:T(8,128)S(1)} reduce(f32[32,1,13824]{2,1,0:T(1,128)S(1)} %all-to-all-done, f32[]{:T(128)} %broadcast.256), dimensions={1}, to_apply=%all_to_all.13.reduce_sub_computation | reduce | bytes 3538948 | tf_op jit(solution)/shard_map/all_to_all | solution.py:82
  134.1 5.3 %reshape.107 = f32[1536,6,48]{2,1,0:T(8,128)} reshape(f32[32,13824]{1,0:T(8,128)S(1)} %reduce.22) | data formatting | bytes 3538944
  139.4 7.7 %copy.19 = f32[48,6,32,48]{0,2,3,1:T(8,128)} copy(f32[48,6,32,48]{0,1,3,2:T(8,128)} %bitcast.75) | data formatting | bytes 3538944 | tf_op jit(solution)/shard_map/all_to_all | solution.py:82
  147.2 5.2 %reshape.99 = f32[1536,288]{0,1:T(8,128)S(1)} reshape(f32[32,48,6,48]{1,0,3,2:T(8,128)} %bitcast.76) | data formatting | bytes 3538944
  152.4 4.0 %fusion.4 = f32[300,288]{0,1:S(1)} fusion(f32[1536,288]{0,1:T(8,128)S(1)} %reshape.99, f32[44,1536]{1,0:T(8,128)S(1)} %copy-done.3, f32[128,1536]{1,0:T(8,128)S(1)} %copy-done.1, f32[128,1536]{1,0:T(8,128)} %fusion.88), kind=kOutput, calls=%fused_computation.13 | convolution fusion | flops 1593446400 | bytes 3958272
  156.5 1.2 fusion.22
  157.7 5.4 %collective-permute-start.1 = (f32[300,4,48]{0,2,1:T(8,128)S(1)}, f32[300,4,48]{0,2,1:T(8,128)S(1)}, u32[]{:S(2)}, u32[]{:S(2)}) collective-permute-start(f32[300,4,48]{0,2,1:T(8,128)S(1)} %get-tuple-element.25), channel_id=1, source_target_pairs={{1,0},{2,1},{3,2},{4,3},{5,4},{6,5},{7,6},{8,7},{9,8},{10,9},{11,1... | collective-permute-start | bytes 691208 | tf_op jit(solution)/shard_map/ppermute | solution.py:19
  163.1 1.9 collective-permute-start
  165.9 3.8 %collective-permute-done.1 = f32[300,4,48]{0,2,1:T(8,128)S(1)} collective-permute-done((f32[300,4,48]{0,2,1:T(8,128)S(1)}, f32[300,4,48]{0,2,1:T(8,128)S(1)}, u32[]{:S(2)}, u32[]{:S(2)}) %collective-permute-start.1) | collective-permute-done | bytes 230432 | tf_op jit(solution)/shard_map/ppermute | solution.py:19
  169.7 6.2 %collective-permute-done = f32[300,4,48]{0,2,1:T(8,128)S(1)} collective-permute-done((f32[300,4,48]{0,2,1:T(8,128)S(1)}, f32[300,4,48]{0,2,1:T(8,128)S(1)}, u32[]{:S(2)}, u32[]{:S(2)}) %collective-permute-start) | collective-permute-done | bytes 230432 | tf_op jit(solution)/shard_map/ppermute | solution.py:18
  175.9 5.8 %fusion.54 = f32[300,6,48]{0,2,1:T(8,128)S(1)} fusion(f32[300,6,48]{0,2,1:T(8,128)S(1)} %bitcast.78, f32[300,4,48]{0,2,1:T(8,128)S(1)} %collective-permute-done.1, f32[300,4,48]{0,2,1:T(8,128)S(1)} %collective-permute-done, f32[6]{0:T(128)S(1)} %select_reduce_fusion.4, f32[]{:T(128)} %bitcast.22, f32[]{:T(128)} %bitcast.21, f32[]{:T(128)} %bitcast.20, ...), kind=kLoop, calls=%fused_computation.101 | loop fusion | flops 2246400 | bytes 1152060 | tf_op jit(solution)/shard_map/div | solution.py:93
  181.7 4.1 %collective-permute-start.3 = (f32[300,6,4]{0,2,1:T(4,128)S(1)}, f32[300,6,4]{0,2,1:T(4,128)S(1)}, u32[]{:S(2)}, u32[]{:S(2)}) collective-permute-start(f32[300,6,4]{0,2,1:T(4,128)S(1)} %get-tuple-element.23), channel_id=1, source_target_pairs={{16,0},{32,16},{48,32},{64,48},{80,64},{96,80},{112,96},{128,112},... | collective-permute-start | bytes 86408 | tf_op jit(solution)/shard_map/ppermute | solution.py:19
  185.8 1.9 collective-permute-start.2
  187.9 6.3 %collective-permute-done.2 = f32[300,6,4]{0,2,1:T(4,128)S(1)} collective-permute-done((f32[300,6,4]{0,2,1:T(4,128)S(1)}, f32[300,6,4]{0,2,1:T(4,128)S(1)}, u32[]{:S(2)}, u32[]{:S(2)}) %collective-permute-start.2) | collective-permute-done | bytes 28832 | tf_op jit(solution)/shard_map/ppermute | solution.py:18
  194.1 6.9 %fusion.33 = f32[300,6,48]{0,2,1:T(8,128)} fusion(f32[300,6,48]{0,2,1:T(8,128)S(1)} %bitcast.79, f32[300,6,48]{0,2,1:T(8,128)S(1)} %fusion.54, f32[300,6,4]{0,2,1:T(4,128)S(1)} %collective-permute-done.3, f32[300,6,4]{0,2,1:T(4,128)S(1)} %collective-permute-done.2, f32[48]{0:T(128)S(1)} %select_reduce_fusion.3, f32[]{:T(128)} %bitcast.22, f32[]{:T(128)} %bitcast.21, ...), kind=kLoop, calls=%fused_computation.80 | loop fusion | flops 2332800 | bytes 1094628 | tf_op jit(solution)/shard_map/sub | solution.py:96
  (64 shorter events, 11.9 us)
Async XLA Ops:
  14.2 12.9 %copy-start.5 = (s32[1536,2]{0,1:T(2,128)S(1)}, s32[1536,2]{0,1:T(2,128)}, u32[]{:S(2)}) copy-start(s32[1536,2]{0,1:T(2,128)} %param.5) | copy-start | bytes 36868
  14.2 114.5 %all-to-all-start = ((f32[32,1,13824]{2,1,0:T(1,128)}), f32[32,1,13824]{2,1,0:T(1,128)S(1)}, u32[]{:S(2)}, u32[]{:S(2)}) async-start(f32[32,1,13824]{2,1,0:T(1,128)} %reshape.106), calls=%async_computation | async-start | bytes 3538944 | tf_op jit(solution)/shard_map/all_to_all | solution.py:82
  124.4 2.5 %copy-start.2 = (f32[44,1536]{1,0:T(8,128)}, f32[44,1536]{1,0:T(8,128)S(1)}, u32[]{:S(2)}) copy-start(f32[44,1536]{1,0:T(8,128)S(1)} %fusion.95) | copy-start | bytes 811012
  126.0 0.9 copy-start
  147.2 5.2 %copy-start.1 = (f32[128,1536]{1,0:T(8,128)S(1)}, f32[128,1536]{1,0:T(8,128)}, u32[]{:S(2)}) copy-start(f32[128,1536]{1,0:T(8,128)} %copy-done) | copy-start | bytes 2359300
  147.2 5.2 %copy-start.3 = (f32[44,1536]{1,0:T(8,128)S(1)}, f32[44,1536]{1,0:T(8,128)}, u32[]{:S(2)}) copy-start(f32[44,1536]{1,0:T(8,128)} %copy-done.2) | copy-start | bytes 811012
  152.4 4.1 %copy-start.6 = (f32[300]{0:T(512)S(1)}, f32[300]{0:T(512)}, u32[]{:S(2)}) copy-start(f32[300]{0:T(512)} %fusion.27) | copy-start | bytes 3604
  156.5 37.7 %copy-start.4 = (f32[300,288]{0,1}, f32[300,288]{0,1:S(1)}, u32[]{:S(2)}) copy-start(f32[300,288]{0,1:S(1)} %fusion.4) | copy-start | bytes 1036804
  157.7 11.9 %collective-permute-start.1 = (f32[300,4,48]{0,2,1:T(8,128)S(1)}, f32[300,4,48]{0,2,1:T(8,128)S(1)}, u32[]{:S(2)}, u32[]{:S(2)}) collective-permute-start(f32[300,4,48]{0,2,1:T(8,128)S(1)} %get-tuple-element.25), channel_id=1, source_target_pairs={{1,0},{2,1},{3,2},{4,3},{5,4},{6,5},{7,6},{8,7},{9,8},{10,9},{11,1... | collective-permute-start | bytes 691208 | tf_op jit(solution)/shard_map/ppermute | solution.py:19
  163.1 12.8 %collective-permute-start = (f32[300,4,48]{0,2,1:T(8,128)S(1)}, f32[300,4,48]{0,2,1:T(8,128)S(1)}, u32[]{:S(2)}, u32[]{:S(2)}) collective-permute-start(f32[300,4,48]{0,2,1:T(8,128)S(1)} %get-tuple-element.24), channel_id=1, source_target_pairs={{0,1},{1,2},{2,3},{3,4},{4,5},{5,6},{6,7},{7,8},{8,9},{9,10},{10,1... | collective-permute-start | bytes 691208 | tf_op jit(solution)/shard_map/ppermute | solution.py:18
  181.7 6.1 %collective-permute-start.3 = (f32[300,6,4]{0,2,1:T(4,128)S(1)}, f32[300,6,4]{0,2,1:T(4,128)S(1)}, u32[]{:S(2)}, u32[]{:S(2)}) collective-permute-start(f32[300,6,4]{0,2,1:T(4,128)S(1)} %get-tuple-element.23), channel_id=1, source_target_pairs={{16,0},{32,16},{48,32},{64,48},{80,64},{96,80},{112,96},{128,112},... | collective-permute-start | bytes 86408 | tf_op jit(solution)/shard_map/ppermute | solution.py:19
  185.8 8.3 %collective-permute-start.2 = (f32[300,6,4]{0,2,1:T(4,128)S(1)}, f32[300,6,4]{0,2,1:T(4,128)S(1)}, u32[]{:S(2)}, u32[]{:S(2)}) collective-permute-start(f32[300,6,4]{0,2,1:T(4,128)S(1)} %get-tuple-element.22), channel_id=1, source_target_pairs={{0,16},{16,32},{32,48},{48,64},{64,80},{80,96},{96,112},{112,128},... | collective-permute-start | bytes 86408 | tf_op jit(solution)/shard_map/ppermute | solution.py:18
where the time goes:
time: 205 us; the launch traced here: 201 us
  other arithmetic  100 us (49%)
  local copies, waits for them, and re-layouts  35.3 us (17%)
  starting transfers between devices  26.2 us (13%)
  matrix products  20 us (10%)
  waiting for transfers between devices  16.2 us (8%)
  between operations  3.26 us (2%)
    another operation x10, other arithmetic, pseudo_inverse(): factor = jnp.linalg.cholesky(normal)  48.7 us
    another operation x7, other arithmetic, pseudo_inverse(): return jax.scipy.linalg.cho_solve((factor, True), design.T)  30.1 us
    unnamed x17, local copies, waits for them, and re-layouts  17.8 us
    all_to_all x1, starting transfers between devices, body(): lax.all_to_all(masked, 'ifg', split_axis=2, concat_axis=0, tiled=True)  12.9 us
    ppermute x2, waiting for transfers between devices, extended(): before = lax.ppermute(last, axis, up)  12.5 us
    ppermute x2, starting transfers between devices, extended(): after = lax.ppermute(leading, axis, down)  9.46 us
    another operation x10, matrix products, pseudo_inverse(): return jax.scipy.linalg.cho_solve((factor, True), design.T)  8.45 us
    all_to_all x2, local copies, waits for them, and re-layouts, body(): lax.all_to_all(masked, 'ifg', split_axis=2, concat_axis=0, tiled=True)  8.33 us
  transfers between devices with their start and end apart: 5, of which 3 were waited for; matrix products, arithmetic and copies ran while one was open for 50% of the time, Pallas kernels for 0%

commit v1 on v0

v1 whole, which is shorter than its diff:
```python
import jax
import jax.numpy as jnp
import numpy as np
from jax import lax
from jax.experimental import pallas as pl
from jax.experimental.pallas import tpu as pltpu
from jax.sharding import PartitionSpec as P

DATES = 300
SPAN = 40
TIME_SIGMA = 6
RIM_WIDTH = 4

DATE_ROWS = 304
DATE_LANES = 384

IFG_COUNT = 32
BAND_COUNT = 16
OWN_IFGS = 48
ROWS = 6
COLS = 48
PIXELS = ROWS * COLS
IFGS = IFG_COUNT * OWN_IFGS

GROUP = 16
GROUPS = OWN_IFGS // GROUP
TAIL = PIXELS - 256
BLOCK = 2 * OWN_IFGS + GROUP
SEND_GROUP = 8
SEND_COLS = SEND_GROUP * COLS

HALO = 512
MIB = 1024 * 1024


def split(value):
    high = value.astype(jnp.bfloat16)
    low = (value - high.astype(jnp.float32)).astype(jnp.bfloat16)
    return high, low


def dot(a, b):
    return jnp.dot(a, b, preferred_element_type=jnp.float32)


def dot_split(a_high, a_low, b_high, b_low):
    return dot(a_high, b_high) + (dot(a_high, b_low) + dot(a_low, b_high))


def pieces(source, target, length):
    while length > 0:
        step = min(length, 128 - source % 128, 128 - target % 128)
        yield source // 128, target // 128, (target - source) % 128, target % 128, target % 128 + step
        source, target, length = source + step, target + step, length - step


def shifted(value, shift):
    return value if shift == 0 else pltpu.roll(value, shift, 1)


def pack_kernel(unwrapped_ref, mask_ref, out_ref):
    lane = lax.broadcasted_iota(jnp.int32, (OWN_IFGS, 128), 1)
    tail_lane = lax.broadcasted_iota(jnp.int32, (GROUP, 128), 1)
    tiles = {}
    for row in range(ROWS):
        for tile in range(SEND_COLS // 128):
            at = (row, slice(None), slice(128 * tile, 128 * tile + 128))
            tiles[row, tile] = unwrapped_ref[at] * mask_ref[at].astype(jnp.float32)
    for dest in range(SEND_GROUP):
        out = [jnp.zeros((OWN_IFGS, 128), jnp.float32) for _ in range(2)]
        tail = jnp.zeros((GROUP, 128), jnp.float32)
        for row in range(ROWS):
            start, target = dest * COLS, row * COLS
            length = min(COLS, 256 - target)
            for source_tile, tile, shift, first, last in pieces(start, target, length):
                moved = shifted(tiles[row, source_tile], shift)
                out[tile] = jnp.where((lane >= first) & (lane < last), moved, out[tile])
            if length < COLS:
                for group in range(GROUPS):
                    for source_tile, _, shift, first, last in pieces(start + length, TAIL * group, COLS - length):
                        moved = shifted(tiles[row, source_tile][GROUP * group : GROUP * (group + 1)], shift)
                        tail = jnp.where((tail_lane >= first) & (tail_lane < last), moved, tail)
        out_ref[dest, 0:OWN_IFGS, :] = out[0]
        out_ref[dest, OWN_IFGS : 2 * OWN_IFGS, :] = out[1]
        out_ref[dest, 2 * OWN_IFGS :, :] = tail


def pack(unwrapped, component_mask):
    block = pl.BlockSpec((ROWS, OWN_IFGS, SEND_COLS), lambda i: (0, 0, i))
    return pl.pallas_call(
        pack_kernel,
        grid=(IFG_COUNT // SEND_GROUP,),
        in_specs=[block, block],
        out_specs=pl.BlockSpec((SEND_GROUP, BLOCK, 128), lambda i: (i, 0, 0)),
        out_shape=jax.ShapeDtypeStruct((IFG_COUNT, BLOCK, 128), jnp.float32),
        compiler_params=pltpu.CompilerParams(vmem_limit_bytes=16 * MIB),
        cost_estimate=pl.CostEstimate(flops=2_000_000, bytes_accessed=5_400_000, transcendentals=0),
        name="mask_pack",
    )(unwrapped, component_mask)


def iota(shape, dim):
    return lax.broadcasted_iota(jnp.int32, shape, dim)


def one_hot(pairs):
    date = iota((DATE_LANES, pairs.shape[1]), 0)
    later = jnp.where(pairs[1:2, :] == date, 1.0, 0.0)
    return (later - jnp.where(pairs[0:1, :] == date, 1.0, 0.0)).astype(jnp.bfloat16)


def identity(rows, cols, first=0):
    return jnp.where(iota((rows, cols), 0) + first == iota((rows, cols), 1), 1.0, 0.0)


def eliminate(normal_ref, band_ref, lower_ref, scaled_ref):
    window = SPAN // 8 + 1
    blocks = DATE_ROWS // 8
    for tile in range(window, window + blocks):
        start = 8 * tile - SPAN
        rows = normal_ref[8 * tile : 8 * tile + 8, :]
        band_ref[8 * tile : 8 * tile + 8, :] = pltpu.roll(rows, (DATE_LANES - start) % DATE_LANES, 1)[:, :128]
    sub = iota((8, 128), 0)
    lane = iota((8, 128), 1)

    def block_step(block, carry):
        left, right = list(carry[:window]), list(carry[window:])
        pivots = jnp.zeros((8, 128), jnp.float32)
        for j in range(8):
            pivot_row = left[0][j : j + 1, :]
            right_row = right[0][j : j + 1, :]
            scale = jnp.broadcast_to(1.0 / pivot_row[:, j : j + 1], (8, 128))
            pivots = jnp.where(sub == j, scale, pivots)
            scaled_row = pivot_row * scale[0:1, :]
            scaled_right = right_row * jnp.concatenate([scale[0:1, :]] * 3, axis=1)
            for q in range(window):
                factor = jnp.broadcast_to(left[q][:, j : j + 1], (8, 128))
                if q == 0:
                    factor = jnp.where(sub > j, factor, 0.0)
                left[q] = left[q] - factor * scaled_row
                right[q] = right[q] - jnp.concatenate([factor] * 3, axis=1) * scaled_right
        at = pl.ds(pl.multiple_of(8 * block, 8), 8)
        lower_ref[at, :] = right[0]
        scaled_ref[at, :] = right[0] * jnp.concatenate([pivots] * 3, axis=1)
        entering = pl.multiple_of(8 * (block + window), 8)
        left = [jnp.where(lane < 120, pltpu.roll(part, 120, 1), 0.0) for part in left[1:]]
        left.append(band_ref[pl.ds(entering, 8), :])
        right = right[1:] + [identity(8, DATE_LANES, entering)]
        return tuple(left + right)

    left = [normal_ref[8 * q : 8 * q + 8, 0:128] for q in range(window)]
    right = [identity(8, DATE_LANES, 8 * q) for q in range(window)]
    lax.fori_loop(0, blocks, block_step, tuple(left + right))


def highpass_matrix():
    row, col = iota((DATE_ROWS, DATE_LANES), 0), iota((DATE_ROWS, DATE_LANES), 1)
    spread = (row - col).astype(jnp.float32)
    weights = jnp.exp(-spread * spread / (2.0 * TIME_SIGMA * TIME_SIGMA))
    weights = jnp.where(col < DATES, weights, 0.0)
    lowpass = weights / jnp.sum(weights, axis=1, keepdims=True)
    return jnp.where((row < DATES) & (col < DATES), identity(DATE_ROWS, DATE_LANES) - lowpass, 0.0)


def tap(offset):
    sigma = RIM_WIDTH / 2.0
    return jnp.where(jnp.abs(offset) <= RIM_WIDTH, jnp.exp(-offset * offset / (2.0 * sigma * sigma)), 0.0)


def operators_kernel(pairs_ref, ordered_ref, target_ref, source_ref, inv_high, inv_low, high_high, high_low,
                     filter_high, filter_low, normal_ref, band_ref, lower_ref, scaled_ref):
    design = one_hot(pairs_ref[...])
    normal = lax.dot_general(design, design, (((1,), (1,)), ((), ())), preferred_element_type=jnp.float32)
    normal_ref[...] = normal + identity(DATE_LANES, DATE_LANES)
    eliminate(normal_ref, band_ref, lower_ref, scaled_ref)
    solve = lax.dot_general(lower_ref[...], scaled_ref[...], (((0,), (0,)), ((), ())),
                            precision=lax.Precision.HIGHEST, preferred_element_type=jnp.float32)
    filtered = jnp.dot(highpass_matrix(), solve, precision=lax.Precision.HIGHEST, preferred_element_type=jnp.float32)
    for matrix, high_ref, low_ref in ((solve[:DATE_ROWS], inv_high, inv_low), (filtered, high_high, high_low)):
        first, second = split(matrix)
        third = (matrix - first.astype(jnp.float32) - second.astype(jnp.float32)).astype(jnp.bfloat16)
        for group in range(GROUPS):
            at = slice(512 * group, 512 * group + 512)
            ordered = one_hot(ordered_ref[:, at])
            product = dot(first, ordered) + (dot(second, ordered) + dot(third, ordered))
            high_ref[:, at], low_ref[:, at] = split(product)
    weights = tap(source_ref[0:1, :] - target_ref[:, 0:1]) * tap(source_ref[1:2, :] - target_ref[:, 1:2])
    filter_high[...], filter_low[...] = split(weights / target_ref[:, 2:3])


def operators(date_pairs, norm):
    pairs = date_pairs.T
    ordered = pairs.reshape(2, IFG_COUNT, GROUPS, GROUP).transpose(0, 2, 1, 3).reshape(2, IFGS)
    row, col = np.divmod(np.arange(PIXELS), COLS)
    target = jnp.concatenate([jnp.asarray(np.stack([row, col], 1), jnp.float32), norm[:, None]], axis=1)
    places = halo_places()
    source_row = np.concatenate([row, np.full(96, 1000), places[0]])
    source_col = np.concatenate([col, np.full(96, 1000), places[1]])
    source = jnp.asarray(np.stack([source_row, source_col]), jnp.float32)
    half = jax.ShapeDtypeStruct((DATE_ROWS, IFGS), jnp.bfloat16)
    weight = jax.ShapeDtypeStruct((PIXELS, DATE_LANES + HALO), jnp.bfloat16)
    whole = pl.BlockSpec(memory_space=pltpu.VMEM)
    return pl.pallas_call(
        operators_kernel,
        in_specs=[whole] * 4,
        out_specs=[whole] * 6,
        out_shape=[half] * 4 + [weight] * 2,
        scratch_shapes=[
            pltpu.VMEM((DATE_LANES, DATE_LANES), jnp.float32),
            pltpu.VMEM((DATE_LANES, 128), jnp.float32),
            pltpu.VMEM((DATE_ROWS, DATE_LANES), jnp.float32),
            pltpu.VMEM((DATE_ROWS, DATE_LANES), jnp.float32),
        ],
        compiler_params=pltpu.CompilerParams(vmem_limit_bytes=32 * MIB),
        cost_estimate=pl.CostEstimate(flops=20_000_000_000, bytes_accessed=5_000_000, transcendentals=0),
        name="operators",
    )(pairs, ordered, target, source)


def project(high_ref, low_ref, data_ref):
    tail = data_ref[:, 2 * OWN_IFGS :, :].reshape(GROUP * IFG_COUNT, 128)
    main, rest = None, None
    for group in range(GROUPS):
        first = data_ref[:, GROUP * group : GROUP * (group + 1), :].reshape(GROUP * IFG_COUNT, 128)
        start = OWN_IFGS + GROUP * group
        second = data_ref[:, start : start + GROUP, :].reshape(GROUP * IFG_COUNT, 128)
        data = split(jnp.concatenate([first, second, tail], axis=1))
        at = slice(512 * group, 512 * group + 512)
        part = dot_split(high_ref[:, at], low_ref[:, at], *data)
        moved = shifted(part[:, 256:], (128 - TAIL * group) % 128)
        main = part[:, :256] if main is None else main + part[:, :256]
        rest = moved if rest is None else rest + moved
    whole = jnp.concatenate([main, rest], axis=1)
    whole = jnp.concatenate([whole, jnp.zeros((DATE_LANES - DATE_ROWS, 384), jnp.float32)], axis=0)
    return whole.T


STEPS = ((0, 1), (0, -1), (1, 0), (-1, 0), (1, 1), (-1, 1), (1, -1), (-1, -1))


def reach(step, length):
    return {1: (length - RIM_WIDTH, length), -1: (0, RIM_WIDTH), 0: (0, length)}[step]


def halo_shape(step):
    (first_col, last_col), (first_row, last_row) = reach(step[0], COLS), reach(step[1], ROWS)
    return range(first_row, last_row), range(first_col, last_col)


def halo_places():
    places = []
    for step in STEPS:
        rows, cols = halo_shape(step)
        places += [(r - ROWS * step[1], c - COLS * step[0]) for r in rows for c in cols]
    places += [(1000, 1000)] * (HALO - len(places))
    return np.array(places).T


def varying_kernel(high_ref, low_ref, data_ref, own_ref, *halo_refs):
    varying = project(high_ref, low_ref, data_ref)
    own_ref[...] = varying[:PIXELS]
    for step, halo_ref in zip(STEPS, halo_refs):
        rows, cols = halo_shape(step)
        for place, row in enumerate(rows):
            first = COLS * row + cols.start
            halo_ref[len(cols) * place : len(cols) * (place + 1), :] = varying[first : first + len(cols)]


def project_varying(high, low, data):
    whole = pl.BlockSpec(memory_space=pltpu.VMEM)
    shapes = [jax.ShapeDtypeStruct((PIXELS, DATE_LANES), jnp.float32)]
    for step in STEPS:
        rows, cols = halo_shape(step)
        shapes.append(jax.ShapeDtypeStruct((len(rows) * len(cols), DATE_LANES), jnp.float32))
    return pl.pallas_call(
        varying_kernel,
        in_specs=[whole] * 3,
        out_specs=[whole] * len(shapes),
        out_shape=shapes,
        compiler_params=pltpu.CompilerParams(vmem_limit_bytes=24 * MIB),
        cost_estimate=pl.CostEstimate(flops=1_100_000_000, bytes_accessed=5_000_000, transcendentals=0),
        name="varying",
    )(high, low, data)


def series_kernel(high_ref, low_ref, data_ref, varying_ref, filter_high, filter_low, series_ref, partial_ref):
    series = project(high_ref, low_ref, data_ref)[:PIXELS]
    for row in range(ROWS):
        series_ref[row] = series[COLS * row : COLS * (row + 1), :DATES]
    own = slice(0, PIXELS)
    smooth = dot_split(filter_high[:, own], filter_low[:, own], *split(varying_ref[...]))
    partial_ref[...] = series - smooth


def project_series(high, low, data, varying, filter_high, filter_low):
    whole = pl.BlockSpec(memory_space=pltpu.VMEM)
    return pl.pallas_call(
        series_kernel,
        in_specs=[whole] * 6,
        out_specs=[whole] * 2,
        out_shape=[
            jax.ShapeDtypeStruct((ROWS, COLS, DATES), jnp.float32),
            jax.ShapeDtypeStruct((PIXELS, DATE_LANES), jnp.float32),
        ],
        compiler_params=pltpu.CompilerParams(vmem_limit_bytes=24 * MIB),
        cost_estimate=pl.CostEstimate(flops=2_000_000_000, bytes_accessed=5_000_000, transcendentals=0),
        name="series",
    )(high, low, data, varying, filter_high, filter_low)


def corrected_kernel(partial_ref, filter_high, filter_low, *refs):
    halo_refs, out_ref = refs[:-1], refs[-1]
    halo = jnp.concatenate([ref[...] for ref in halo_refs], axis=0)
    halo = jnp.concatenate([halo, jnp.zeros((HALO - halo.shape[0], DATE_LANES), jnp.float32)], axis=0)
    at = slice(DATE_LANES, DATE_LANES + HALO)
    result = partial_ref[...] - dot_split(filter_high[:, at], filter_low[:, at], *split(halo))
    for row in range(ROWS):
        out_ref[row] = result[COLS * row : COLS * (row + 1), :DATES]


def correct(partial, filter_high, filter_low, halos):
    whole = pl.BlockSpec(memory_space=pltpu.VMEM)
    return pl.pallas_call(
        corrected_kernel,
        in_specs=[whole] * (3 + len(halos)),
        out_specs=whole,
        out_shape=jax.ShapeDtypeStruct((ROWS, COLS, DATES), jnp.float32),
        compiler_params=pltpu.CompilerParams(vmem_limit_bytes=16 * MIB),
        cost_estimate=pl.CostEstimate(flops=500_000_000, bytes_accessed=3_000_000, transcendentals=0),
        name="corrected",
    )(partial, filter_high, filter_low, *halos)


def passed(value, step):
    pairs = []
    for i in range(IFG_COUNT):
        for b in range(BAND_COUNT):
            to_i, to_b = i + step[0], b + step[1]
            if 0 <= to_i < IFG_COUNT and 0 <= to_b < BAND_COUNT:
                pairs.append((i * BAND_COUNT + b, to_i * BAND_COUNT + to_b))
    return lax.ppermute(value, ("ifg", "band"), pairs)


def edge_weights(start, count, total):
    offsets = jnp.arange(-RIM_WIDTH, RIM_WIDTH + 1, dtype=jnp.int32)
    places = start + jnp.arange(count, dtype=jnp.int32)[:, None] + offsets[None, :]
    inside = ((places >= 0) & (places < total)).astype(jnp.float32)
    return jnp.sum(inside * tap(offsets.astype(jnp.float32))[None, :], axis=1)


def body(unwrapped, component_mask, date_pairs):
    blocks = pack(unwrapped.transpose(1, 0, 2), component_mask.transpose(1, 0, 2))
    data = lax.all_to_all(blocks, "ifg", split_axis=0, concat_axis=0, tiled=True)
    row_norm = edge_weights(lax.axis_index("band") * ROWS, ROWS, ROWS * BAND_COUNT)
    column_norm = edge_weights(lax.axis_index("ifg") * COLS, COLS, COLS * IFG_COUNT)
    norm = (row_norm[:, None] * column_norm[None, :]).reshape(PIXELS)
    inv_high, inv_low, high_high, high_low, filter_high, filter_low = operators(date_pairs, norm)
    varying, *edges = project_varying(high_high, high_low, data)
    halos = [passed(edge, step) for edge, step in zip(edges, STEPS)]
    series, partial = project_series(inv_high, inv_low, data, varying, filter_high, filter_low)
    corrected = correct(partial, filter_high, filter_low, halos)
    return series.transpose(2, 0, 1), corrected.transpose(2, 0, 1)


def solution(mesh):
    placed = (P("ifg", "band", None), P("ifg", "band", None), P())
    return jax.shard_map(
        body,
        mesh=mesh,
        in_specs=placed,
        out_specs=(P(None, "band", "ifg"), P(None, "band", "ifg")),
        check_vma=False,
    )
```

time: 205 us -> 110 us (0.54)
  the two profiles are of different devices: /device:TPU:66 before, /device:TPU:70 now
where the time goes in v1:
time: 110 us; the launch traced here: 109 us
  starting transfers between devices  49.5 us (45%)
  Pallas kernels  44.1 us (40%)
  local copies, waits for them, and re-layouts  9.55 us (9%)
  waiting for transfers between devices  4.9 us (4%)
    ppermute x8, starting transfers between devices, passed(): return lax.ppermute(value, ('ifg', 'band'), pairs)  36.8 us
    pallas_call x1, Pallas kernels, operators(): pl.pallas_call(operators_kernel, in_specs=[whole] * 4, out_specs=[whole]...  35.1 us
    all_to_all x1, starting transfers between devices, body(): lax.all_to_all(blocks, 'ifg', split_axis=0, concat_axis=0, tiled=True)  12.7 us
    unnamed x26, local copies, waits for them, and re-layouts  9.08 us
    all_to_all x1, waiting for transfers between devices, body(): lax.all_to_all(blocks, 'ifg', split_axis=0, concat_axis=0, tiled=True)  4.14 us
    pallas_call x1, Pallas kernels, pack(): pl.pallas_call(pack_kernel, grid=(IFG_COUNT // SEND_GROUP,), in_specs=[bl...  3.01 us
    pallas_call x1, Pallas kernels, project_series(): pl.pallas_call(series_kernel, in_specs=[whole] * 6, out_specs=[whole] * 2...  2.72 us
  transfers between devices with their start and end apart: 9, of which 2 were waited for; matrix products, arithmetic and copies ran while one was open for 1% of the time, Pallas kernels for 35%

profile of v1, /device:TPU:70, one launch (start us, length us, event | category | flops | bytes accessed | tf_op | source)
XLA Modules:
  0.0 109.3 jit_solution(14223128118776070993)
XLA Ops:
  0.6 1.5 %copy-done = f32[48,6,1536]{2,0,1:T(8,128)S(1)} copy-done((f32[48,6,1536]{2,0,1:T(8,128)S(1)}, f32[48,6,1536]{2,0,1:T(8,128)}, u32[]{:S(2)}) %copy-start) | copy-done | bytes 1769496
  2.1 1.5 %copy-done.1 = s32[48,6,1536]{2,0,1:T(8,128)S(1)} copy-done((s32[48,6,1536]{2,0,1:T(8,128)S(1)}, s32[48,6,1536]{2,0,1:T(8,128)}, u32[]{:S(2)}) %copy-start.1) | copy-done | bytes 1769496
  3.6 3.0 %mask_pack.1 = f32[32,112,128]{2,1,0:T(8,128)} custom-call(f32[6,48,1536]{2,1,0:T(8,128)S(1)} %bitcast.8, s32[6,48,1536]{2,1,0:T(8,128)S(1)} %bitcast.9), custom_call_target="tpu_custom_call" | custom-call | flops 2000000 | bytes 5400000 | tf_op jit(solution)/shard_map/mask_pack/pallas_call | solution.py:90
  6.6 12.7 %all-to-all-start = ((f32[32,112,128]{2,1,0:T(8,128)}), f32[32,112,128]{2,1,0:T(8,128)S(1)}, u32[]{:S(2)}, u32[]{:S(2)}) async-start(f32[32,112,128]{2,1,0:T(8,128)} %mask_pack.1), calls=%async_computation | async-start | bytes 3670016 | tf_op jit(solution)/shard_map/all_to_all | solution.py:353
  19.3 0.2 select_reduce_fusion.1
  19.5 0.1 select_reduce_fusion
  19.6 0.1 broadcast_multiply_fusion
  19.7 0.1 mul.65
  19.8 0.1 reshape.58
  19.9 0.1 reshape.59.ordered_ref
  20.1 0.1 copy.13.target_ref
  20.2 35.1 %operators.1 = (bf16[304,1536]{1,0:T(8,128)(2,1)S(1)}, bf16[304,1536]{1,0:T(8,128)(2,1)S(1)}, bf16[304,1536]{1,0:T(8,128)(2,1)S(1)}, bf16[304,1536]{1,0:T(8,128)...) custom-call(s32[2,1536]{1,0:T(2,128)S(1)} %bitcast.11, s32[2,1536]{1,0:T(2,128)S(1)} %reshape.59.ordered_ref, ...), custom_call_target="tpu_custom_call" | custom-call | flops 20000000000 | bytes 5000000 | tf_op jit(solution)/shard_map/operators/pallas_call | solution.py:203
  55.3 0.9 copy-done.4
  56.2 0.9 copy-done.6
  57.2 0.9 copy-done.8
  58.1 0.9 copy-done.10
  59.1 4.1 %all-to-all-done.data_ref = f32[32,112,128]{2,1,0:T(8,128)S(1)} async-done(((f32[32,112,128]{2,1,0:T(8,128)}), f32[32,112,128]{2,1,0:T(8,128)S(1)}, u32[]{:S(2)}, u32[]{:S(2)}) %all-to-all-start) | async-done | bytes 1835040 | tf_op jit(solution)/shard_map/all_to_all | solution.py:353
  63.2 1.2 %copy-done.5 = bf16[304,1536]{1,0:T(8,128)(2,1)S(1)} copy-done((bf16[304,1536]{1,0:T(8,128)(2,1)S(1)}, bf16[304,1536]{1,0:T(8,128)(2,1)}, u32[]{:S(2)}) %copy-start.5) | copy-done | bytes 933912
  64.4 1.2 %copy-done.7 = bf16[304,1536]{1,0:T(8,128)(2,1)S(1)} copy-done((bf16[304,1536]{1,0:T(8,128)(2,1)S(1)}, bf16[304,1536]{1,0:T(8,128)(2,1)}, u32[]{:S(2)}) %copy-start.7) | copy-done | bytes 933912
  65.6 1.9 %varying.1 = (f32[288,384]{1,0:T(8,128)S(1)}, f32[192,384]{1,0:T(8,128)S(1)}, f32[192,384]{1,0:T(8,128)S(1)}, f32[24,384]{1,0:T(8,128)S(1)}, f32[24,384]{1,0:T(8...) custom-call(bf16[304,1536]{1,0:T(8,128)(2,1)S(1)} %copy-done.5, ...), custom_call_target="tpu_custom_call" | custom-call | flops 1100000000 | bytes 5000000 | tf_op jit(solution)/shard_map/varying/pallas_call | solution.py:275
  67.5 3.5 %collective-permute-start = (f32[192,384]{1,0:T(8,128)S(1)}, f32[192,384]{1,0:T(8,128)S(1)}, u32[]{:S(2)}, u32[]{:S(2)}) collective-permute-start(f32[192,384]{1,0:T(8,128)S(1)} %get-tuple-element.28), channel_id=1, source_target_pairs={{0,1},{1,2},{2,3},{3,4},{4,5},{5,6},{6,7},{7,8},{8,9},{9,10},{10,1... | collective-permute-start | bytes 884744 | tf_op jit(solution)/shard_map/ppermute | solution.py:341
  71.0 4.5 %collective-permute-start.1 = (f32[192,384]{1,0:T(8,128)S(1)}, f32[192,384]{1,0:T(8,128)S(1)}, u32[]{:S(2)}, u32[]{:S(2)}) collective-permute-start(f32[192,384]{1,0:T(8,128)S(1)} %get-tuple-element.29), channel_id=1, source_target_pairs={{1,0},{2,1},{3,2},{4,3},{5,4},{6,5},{7,6},{8,7},{9,8},{10,9},{11,1... | collective-permute-start | bytes 884744 | tf_op jit(solution)/shard_map/ppermute | solution.py:341
  75.4 1.9 %collective-permute-start.4 = (f32[16,384]{1,0:T(8,128)S(1)}, f32[16,384]{1,0:T(8,128)S(1)}, u32[]{:S(2)}, u32[]{:S(2)}) collective-permute-start(f32[16,384]{1,0:T(8,128)S(1)} %get-tuple-element.32), channel_id=1, source_target_pairs={{0,17},{1,18},{2,19},{3,20},{4,21},{5,22},{6,23},{7,24},{8,25},{9,... | collective-permute-start | bytes 73736 | tf_op jit(solution)/shard_map/ppermute | solution.py:341
  77.4 6.6 %collective-permute-start.5 = (f32[16,384]{1,0:T(8,128)S(1)}, f32[16,384]{1,0:T(8,128)S(1)}, u32[]{:S(2)}, u32[]{:S(2)}) collective-permute-start(f32[16,384]{1,0:T(8,128)S(1)} %get-tuple-element.33), channel_id=1, source_target_pairs={{16,1},{17,2},{18,3},{19,4},{20,5},{21,6},{22,7},{23,8},{24,9},{25... | collective-permute-start | bytes 73736 | tf_op jit(solution)/shard_map/ppermute | solution.py:341
  83.9 2.1 %collective-permute-start.6 = (f32[16,384]{1,0:T(8,128)S(1)}, f32[16,384]{1,0:T(8,128)S(1)}, u32[]{:S(2)}, u32[]{:S(2)}) collective-permute-start(f32[16,384]{1,0:T(8,128)S(1)} %get-tuple-element.34), channel_id=1, source_target_pairs={{1,16},{2,17},{3,18},{4,19},{5,20},{6,21},{7,22},{8,23},{9,24},{10... | collective-permute-start | bytes 73736 | tf_op jit(solution)/shard_map/ppermute | solution.py:341
  86.0 0.7 collective-permute-done.4.refs_4_
  86.8 9.8 %collective-permute-start.7 = (f32[16,384]{1,0:T(8,128)S(1)}, f32[16,384]{1,0:T(8,128)S(1)}, u32[]{:S(2)}, u32[]{:S(2)}) collective-permute-start(f32[16,384]{1,0:T(8,128)S(1)} %get-tuple-element.35), channel_id=1, source_target_pairs={{17,0},{18,1},{19,2},{20,3},{21,4},{22,5},{23,6},{24,7},{25,8},{26... | collective-permute-start | bytes 73736 | tf_op jit(solution)/shard_map/ppermute | solution.py:341
  96.5 1.9 %collective-permute-start.2 = (f32[24,384]{1,0:T(8,128)S(1)}, f32[24,384]{1,0:T(8,128)S(1)}, u32[]{:S(2)}, u32[]{:S(2)}) collective-permute-start(f32[24,384]{1,0:T(8,128)S(1)} %get-tuple-element.30), channel_id=1, source_target_pairs={{0,16},{1,17},{2,18},{3,19},{4,20},{5,21},{6,22},{7,23},{8,24},{9,... | collective-permute-start | bytes 110600 | tf_op jit(solution)/shard_map/ppermute | solution.py:341
  98.5 6.7 %collective-permute-start.3 = (f32[24,384]{1,0:T(8,128)S(1)}, f32[24,384]{1,0:T(8,128)S(1)}, u32[]{:S(2)}, u32[]{:S(2)}) collective-permute-start(f32[24,384]{1,0:T(8,128)S(1)} %get-tuple-element.31), channel_id=1, source_target_pairs={{16,0},{17,1},{18,2},{19,3},{20,4},{21,5},{22,6},{23,7},{24,8},{25... | collective-permute-start | bytes 110600 | tf_op jit(solution)/shard_map/ppermute | solution.py:341
  105.1 2.7 %series.1 = (f32[6,48,300]{2,1,0:T(8,128)}, f32[288,384]{1,0:T(8,128)S(1)}) custom-call(bf16[304,1536]{1,0:T(8,128)(2,1)S(1)} %copy-done.9, bf16[304,1536]{1,0:T(8,128)(2,1)S(1)} %copy-done.11, f32[32,112,128]{2,1,0:T(8,128)S(1)} %all-to-all-done.data_ref, f32[288,384]{1,0:T(8,128)S(1)} %get-tuple-element.23.varying_ref, ...), custom_call_target="tpu_custom_call" | custom-call | flops 2000000000 | bytes 5000000 | tf_op jit(solution)/shard_map/series/pallas_call | solution.py:297
  107.9 0.0 collective-permute-done.7.refs_7_
  107.9 1.4 %corrected.1 = f32[6,48,300]{2,1,0:T(8,128)} custom-call(f32[288,384]{1,0:T(8,128)S(1)} %get-tuple-element.27.partial_ref, bf16[288,896]{1,0:T(8,128)(2,1)S(1)} %get-tuple-element.24.filter_high, bf16[288,896]{1,0:T(8,128)(2,1)S(1)} %get-tuple-element.25.filter_low, f32[192,384]{1,0:T(8,128)S(1)} %collective-permute-done.refs_0_, ...), custom_call_target="tpu_custom_call" | custom-call | flops 500000000 | bytes 3000000 | tf_op jit(solution)/shard_map/corrected/pallas_call | solution.py:323
  (30 shorter events, 0.1 us)
Async XLA Ops:
  0.6 1.5 %copy-start = (f32[48,6,1536]{2,0,1:T(8,128)S(1)}, f32[48,6,1536]{2,0,1:T(8,128)}, u32[]{:S(2)}) copy-start(f32[48,6,1536]{2,0,1:T(8,128)} %param.5) | copy-start | bytes 5308420
  2.1 1.5 %copy-start.1 = (s32[48,6,1536]{2,0,1:T(8,128)S(1)}, s32[48,6,1536]{2,0,1:T(8,128)}, u32[]{:S(2)}) copy-start(s32[48,6,1536]{2,0,1:T(8,128)} %param.6) | copy-start | bytes 5308420
  6.6 13.2 %copy-start.2 = (s32[1536,2]{0,1:T(2,128)S(1)}, s32[1536,2]{0,1:T(2,128)}, u32[]{:S(2)}) copy-start(s32[1536,2]{0,1:T(2,128)} %param.7) | copy-start | bytes 36868
  6.6 13.4 %copy-start.12 = (f32[288,2]{0,1:T(2,128)S(1)}, f32[288,2]{0,1:T(2,128)}, u32[]{:S(2)}) copy-start(f32[288,2]{0,1:T(2,128)} %constant.35.clone) | copy-start | bytes 6916
  6.6 13.6 %copy-start.3 = (f32[2,896]{1,0:T(2,128)S(1)}, f32[2,896]{1,0:T(2,128)}, u32[]{:S(2)}) copy-start(f32[2,896]{1,0:T(2,128)} %constant.36.clone.source_ref) | copy-start | bytes 21508
  6.6 56.6 %all-to-all-start = ((f32[32,112,128]{2,1,0:T(8,128)}), f32[32,112,128]{2,1,0:T(8,128)S(1)}, u32[]{:S(2)}, u32[]{:S(2)}) async-start(f32[32,112,128]{2,1,0:T(8,128)} %mask_pack.1), calls=%async_computation | async-start | bytes 3670016 | tf_op jit(solution)/shard_map/all_to_all | solution.py:353
  55.3 0.9 copy-start.4
  56.2 0.9 copy-start.6
  57.2 0.9 copy-start.8
  58.1 0.9 copy-start.10
  63.2 1.2 %copy-start.5 = (bf16[304,1536]{1,0:T(8,128)(2,1)S(1)}, bf16[304,1536]{1,0:T(8,128)(2,1)}, u32[]{:S(2)}) copy-start(bf16[304,1536]{1,0:T(8,128)(2,1)} %copy-done.4) | copy-start | bytes 2801668
  64.4 1.2 %copy-start.7 = (bf16[304,1536]{1,0:T(8,128)(2,1)S(1)}, bf16[304,1536]{1,0:T(8,128)(2,1)}, u32[]{:S(2)}) copy-start(bf16[304,1536]{1,0:T(8,128)(2,1)} %copy-done.6) | copy-start | bytes 2801668
  65.6 39.6 %copy-start.9 = (bf16[304,1536]{1,0:T(8,128)(2,1)S(1)}, bf16[304,1536]{1,0:T(8,128)(2,1)}, u32[]{:S(2)}) copy-start(bf16[304,1536]{1,0:T(8,128)(2,1)} %copy-done.8) | copy-start | bytes 2801668
  65.6 39.6 %copy-start.11 = (bf16[304,1536]{1,0:T(8,128)(2,1)S(1)}, bf16[304,1536]{1,0:T(8,128)(2,1)}, u32[]{:S(2)}) copy-start(bf16[304,1536]{1,0:T(8,128)(2,1)} %copy-done.10) | copy-start | bytes 2801668
  67.5 40.4 %collective-permute-start = (f32[192,384]{1,0:T(8,128)S(1)}, f32[192,384]{1,0:T(8,128)S(1)}, u32[]{:S(2)}, u32[]{:S(2)}) collective-permute-start(f32[192,384]{1,0:T(8,128)S(1)} %get-tuple-element.28), channel_id=1, source_target_pairs={{0,1},{1,2},{2,3},{3,4},{4,5},{5,6},{6,7},{7,8},{8,9},{9,10},{10,1... | collective-permute-start | bytes 884744 | tf_op jit(solution)/shard_map/ppermute | solution.py:341
  71.0 36.9 %collective-permute-start.1 = (f32[192,384]{1,0:T(8,128)S(1)}, f32[192,384]{1,0:T(8,128)S(1)}, u32[]{:S(2)}, u32[]{:S(2)}) collective-permute-start(f32[192,384]{1,0:T(8,128)S(1)} %get-tuple-element.29), channel_id=1, source_target_pairs={{1,0},{2,1},{3,2},{4,3},{5,4},{6,5},{7,6},{8,7},{9,8},{10,9},{11,1... | collective-permute-start | bytes 884744 | tf_op jit(solution)/shard_map/ppermute | solution.py:341
  75.4 11.3 %collective-permute-start.4 = (f32[16,384]{1,0:T(8,128)S(1)}, f32[16,384]{1,0:T(8,128)S(1)}, u32[]{:S(2)}, u32[]{:S(2)}) collective-permute-start(f32[16,384]{1,0:T(8,128)S(1)} %get-tuple-element.32), channel_id=1, source_target_pairs={{0,17},{1,18},{2,19},{3,20},{4,21},{5,22},{6,23},{7,24},{8,25},{9,... | collective-permute-start | bytes 73736 | tf_op jit(solution)/shard_map/ppermute | solution.py:341
  77.4 19.2 %collective-permute-start.5 = (f32[16,384]{1,0:T(8,128)S(1)}, f32[16,384]{1,0:T(8,128)S(1)}, u32[]{:S(2)}, u32[]{:S(2)}) collective-permute-start(f32[16,384]{1,0:T(8,128)S(1)} %get-tuple-element.33), channel_id=1, source_target_pairs={{16,1},{17,2},{18,3},{19,4},{20,5},{21,6},{22,7},{23,8},{24,9},{25... | collective-permute-start | bytes 73736 | tf_op jit(solution)/shard_map/ppermute | solution.py:341
  83.9 14.5 %collective-permute-start.6 = (f32[16,384]{1,0:T(8,128)S(1)}, f32[16,384]{1,0:T(8,128)S(1)}, u32[]{:S(2)}, u32[]{:S(2)}) collective-permute-start(f32[16,384]{1,0:T(8,128)S(1)} %get-tuple-element.34), channel_id=1, source_target_pairs={{1,16},{2,17},{3,18},{4,19},{5,20},{6,21},{7,22},{8,23},{9,24},{10... | collective-permute-start | bytes 73736 | tf_op jit(solution)/shard_map/ppermute | solution.py:341
  86.8 21.1 %collective-permute-start.7 = (f32[16,384]{1,0:T(8,128)S(1)}, f32[16,384]{1,0:T(8,128)S(1)}, u32[]{:S(2)}, u32[]{:S(2)}) collective-permute-start(f32[16,384]{1,0:T(8,128)S(1)} %get-tuple-element.35), channel_id=1, source_target_pairs={{17,0},{18,1},{19,2},{20,3},{21,4},{22,5},{23,6},{24,7},{25,8},{26... | collective-permute-start | bytes 73736 | tf_op jit(solution)/shard_map/ppermute | solution.py:341
  96.5 11.3 %collective-permute-start.2 = (f32[24,384]{1,0:T(8,128)S(1)}, f32[24,384]{1,0:T(8,128)S(1)}, u32[]{:S(2)}, u32[]{:S(2)}) collective-permute-start(f32[24,384]{1,0:T(8,128)S(1)} %get-tuple-element.30), channel_id=1, source_target_pairs={{0,16},{1,17},{2,18},{3,19},{4,20},{5,21},{6,22},{7,23},{8,24},{9,... | collective-permute-start | bytes 110600 | tf_op jit(solution)/shard_map/ppermute | solution.py:341
  98.5 9.4 %collective-permute-start.3 = (f32[24,384]{1,0:T(8,128)S(1)}, f32[24,384]{1,0:T(8,128)S(1)}, u32[]{:S(2)}, u32[]{:S(2)}) collective-permute-start(f32[24,384]{1,0:T(8,128)S(1)} %get-tuple-element.31), channel_id=1, source_target_pairs={{16,0},{17,1},{18,2},{19,3},{20,4},{21,5},{22,6},{23,7},{24,8},{25... | collective-permute-start | bytes 110600 | tf_op jit(solution)/shard_map/ppermute | solution.py:341

commit v2 on v1

v2 whole, which is shorter than its diff:
```python
import jax
import jax.numpy as jnp
import numpy as np
from jax import lax
from jax.experimental import pallas as pl
from jax.experimental.pallas import tpu as pltpu
from jax.sharding import PartitionSpec as P

DATES = 300
SPAN = 40
TIME_SIGMA = 6
RIM_WIDTH = 4

DATE_ROWS = 304
DATE_LANES = 384

IFG_COUNT = 32
BAND_COUNT = 16
OWN_IFGS = 48
ROWS = 6
COLS = 48
PIXELS = ROWS * COLS
IFGS = IFG_COUNT * OWN_IFGS

WIDE = COLS + 2 * RIM_WIDTH
WIDE_PIXELS = ROWS * WIDE
LANES = 384

GROUP = 16
GROUPS = OWN_IFGS // GROUP
TAIL = WIDE_PIXELS - 256
SPARE = 128 - TAIL
BLOCK = 2 * OWN_IFGS + 2 * GROUP
SEND_GROUP = 8
SEND_COLS = SEND_GROUP * COLS
SEND_TILES = SEND_COLS // 128

EDGE_PIXELS = RIM_WIDTH * COLS
EDGE_ROWS = 2 * EDGE_PIXELS + EDGE_PIXELS // 2
MIB = 1024 * 1024
WHOLE = pl.BlockSpec(memory_space=pltpu.VMEM)


def split(value):
    high = value.astype(jnp.bfloat16)
    low = (value - high.astype(jnp.float32)).astype(jnp.bfloat16)
    return high, low


def dot(a, b):
    return jnp.dot(a, b, preferred_element_type=jnp.float32)


def full_dot(a, b):
    return jnp.dot(a, b, precision=lax.Precision.HIGHEST, preferred_element_type=jnp.float32)


def pieces(source, target, length):
    while length > 0:
        step = min(length, 128 - source % 128, 128 - target % 128)
        yield source // 128, target // 128, (target - source) % 128, target % 128, target % 128 + step
        source, target, length = source + step, target + step, length - step


def shifted(value, shift):
    return value if shift == 0 else pltpu.roll(value, shift, 1)


def tail_runs(group, source, pixel, length):
    for first, last, base in ((0, TAIL, 128 * group),) if group < 2 else ((0, SPARE, TAIL), (SPARE, TAIL, 128 + TAIL)):
        start, stop = max(pixel, first), min(pixel + length, last)
        if start < stop:
            yield source + start - pixel, base + start - first, stop - start


def pack_kernel(*refs):
    (before, inner, after), out_ref = zip(refs[0:3], refs[3:6]), refs[6]
    step = pl.program_id(0)
    lane = lax.broadcasted_iota(jnp.int32, (OWN_IFGS, 128), 1)
    tail_lane = lax.broadcasted_iota(jnp.int32, (GROUP, 128), 1)

    def masked(pair, row, tile):
        at = (row, slice(None), slice(128 * tile, 128 * tile + 128))
        return pair[0][at] * pair[1][at].astype(jnp.float32)

    tiles = {}
    for row in range(ROWS):
        tiles[row, -1] = jnp.where(step > 0, masked(before, row, 0), 0.0)
        for tile in range(SEND_TILES):
            tiles[row, tile] = masked(inner, row, tile)
        tiles[row, SEND_TILES] = jnp.where(step < pl.num_programs(0) - 1, masked(after, row, 0), 0.0)
    for dest in range(SEND_GROUP):
        out = [jnp.zeros((OWN_IFGS, 128), jnp.float32) for _ in range(2)]
        tail = [jnp.zeros((GROUP, 128), jnp.float32) for _ in range(2)]
        for row in range(ROWS):
            source, target = dest * COLS - RIM_WIDTH, row * WIDE
            length = min(max(256 - target, 0), WIDE)
            for source_tile, tile, shift, first, last in pieces(source, target, length):
                moved = shifted(tiles[row, source_tile], shift)
                out[tile] = jnp.where((lane >= first) & (lane < last), moved, out[tile])
            for group in range(GROUPS):
                for run in tail_runs(group, source + length, target + length - 256, WIDE - length):
                    for source_tile, tile, shift, first, last in pieces(*run):
                        moved = shifted(tiles[row, source_tile][GROUP * group : GROUP * (group + 1)], shift)
                        tail[tile] = jnp.where((tail_lane >= first) & (tail_lane < last), moved, tail[tile])
        out_ref[dest, 0:OWN_IFGS, :] = out[0]
        out_ref[dest, OWN_IFGS : 2 * OWN_IFGS, :] = out[1]
        out_ref[dest, 2 * OWN_IFGS : 2 * OWN_IFGS + GROUP, :] = tail[0]
        out_ref[dest, 2 * OWN_IFGS + GROUP :, :] = tail[1]


def pack(unwrapped, component_mask):
    steps = IFG_COUNT // SEND_GROUP
    last = SEND_TILES * steps - 1
    tile = (ROWS, OWN_IFGS, 128)
    blocks = [
        pl.BlockSpec(tile, lambda i: (0, 0, jnp.maximum(SEND_TILES * i - 1, 0))),
        pl.BlockSpec((ROWS, OWN_IFGS, SEND_COLS), lambda i: (0, 0, i)),
        pl.BlockSpec(tile, lambda i: (0, 0, jnp.minimum(SEND_TILES * (i + 1), last))),
    ]
    return pl.pallas_call(
        pack_kernel,
        grid=(steps,),
        in_specs=blocks + blocks,
        out_specs=pl.BlockSpec((SEND_GROUP, BLOCK, 128), lambda i: (i, 0, 0)),
        out_shape=jax.ShapeDtypeStruct((IFG_COUNT, BLOCK, 128), jnp.float32),
        compiler_params=pltpu.CompilerParams(vmem_limit_bytes=56 * MIB),
        cost_estimate=pl.CostEstimate(flops=2_000_000, bytes_accessed=5_600_000, transcendentals=0),
        name="mask_pack",
    )(*[unwrapped] * 3, *[component_mask] * 3)


def iota(shape, dim):
    return lax.broadcasted_iota(jnp.int32, shape, dim)


def one_hot(pairs, dates):
    date = iota((dates, pairs.shape[1]), 0)
    later = jnp.where(pairs[1:2, :] == date, 1.0, 0.0)
    return (later - jnp.where(pairs[0:1, :] == date, 1.0, 0.0)).astype(jnp.bfloat16)


def identity(rows, cols, first=0):
    return jnp.where(iota((rows, cols), 0) + first == iota((rows, cols), 1), 1.0, 0.0)


def eliminate(normal_ref, band_ref, lower_ref, scaled_ref):
    window = SPAN // 8 + 1
    blocks = DATE_ROWS // 8
    for tile in range(window, window + blocks):
        start = 8 * tile - SPAN
        rows = normal_ref[8 * tile : 8 * tile + 8, :]
        band_ref[8 * tile : 8 * tile + 8, :] = pltpu.roll(rows, (DATE_LANES - start) % DATE_LANES, 1)[:, :128]
    sub = iota((8, 128), 0)
    lane = iota((8, 128), 1)

    def block_step(block, carry):
        left, right = list(carry[:window]), list(carry[window:])
        pivots = jnp.zeros((8, 128), jnp.float32)
        for j in range(8):
            pivot_row = left[0][j : j + 1, :]
            right_row = right[0][j : j + 1, :]
            scale = jnp.broadcast_to(1.0 / pivot_row[:, j : j + 1], (8, 128))
            pivots = jnp.where(sub == j, scale, pivots)
            scaled_row = pivot_row * scale[0:1, :]
            scaled_right = right_row * jnp.concatenate([scale[0:1, :]] * 3, axis=1)
            for q in range(window):
                factor = jnp.broadcast_to(left[q][:, j : j + 1], (8, 128))
                if q == 0:
                    factor = jnp.where(sub > j, factor, 0.0)
                left[q] = left[q] - factor * scaled_row
                right[q] = right[q] - jnp.concatenate([factor] * 3, axis=1) * scaled_right
        at = pl.ds(pl.multiple_of(8 * block, 8), 8)
        lower_ref[at, :] = right[0]
        scaled_ref[at, :] = right[0] * jnp.concatenate([pivots] * 3, axis=1)
        entering = pl.multiple_of(8 * (block + window), 8)
        left = [jnp.where(lane < 120, pltpu.roll(part, 120, 1), 0.0) for part in left[1:]]
        left.append(band_ref[pl.ds(entering, 8), :])
        right = right[1:] + [identity(8, DATE_LANES, entering)]
        return tuple(left + right)

    left = [normal_ref[8 * q : 8 * q + 8, 0:128] for q in range(window)]
    right = [identity(8, DATE_LANES, 8 * q) for q in range(window)]
    lax.fori_loop(0, blocks, block_step, tuple(left + right))


def highpass_matrix():
    row, col = iota((DATE_ROWS, DATE_LANES), 0), iota((DATE_ROWS, DATE_LANES), 1)
    spread = (row - col).astype(jnp.float32)
    weights = jnp.exp(-spread * spread / (2.0 * TIME_SIGMA * TIME_SIGMA))
    weights = jnp.where(col < DATES, weights, 0.0)
    lowpass = weights / jnp.sum(weights, axis=1, keepdims=True)
    return jnp.where((row < DATES) & (col < DATES), identity(DATE_ROWS, DATE_LANES) - lowpass, 0.0)


def tap(offset):
    sigma = RIM_WIDTH / 2.0
    return jnp.where(jnp.abs(offset) <= RIM_WIDTH, jnp.exp(-offset * offset / (2.0 * sigma * sigma)), 0.0)


def operators_kernel(pairs_ref, target_ref, source_ref, solve_ref, filtered_ref, filter_high, filter_low,
                     normal_ref, band_ref, lower_ref, scaled_ref):
    design = one_hot(pairs_ref[...], DATE_LANES)
    normal = lax.dot_general(design, design, (((1,), (1,)), ((), ())), preferred_element_type=jnp.float32)
    normal_ref[...] = normal + identity(DATE_LANES, DATE_LANES)
    eliminate(normal_ref, band_ref, lower_ref, scaled_ref)
    solve = lax.dot_general(lower_ref[...], scaled_ref[...], (((0,), (0,)), ((), ())),
                            precision=lax.Precision.HIGHEST, preferred_element_type=jnp.float32)
    solve_ref[...] = solve[:DATE_ROWS]
    filtered_ref[...] = full_dot(highpass_matrix(), solve)
    same_row = source_ref[:, 0:1] == target_ref[0:1, :]
    weights = tap(source_ref[:, 1:2] - target_ref[1:2, :]) / target_ref[2:3, :]
    filter_high[...], filter_low[...] = split(jnp.where(same_row, weights, 0.0))


def operators(pairs, column_norm):
    row, col = np.divmod(np.arange(PIXELS), COLS)
    place = np.stack([np.append(row, np.full(LANES - PIXELS, 2000)), np.append(col, np.zeros(LANES - PIXELS))])
    norm = jnp.concatenate([jnp.tile(column_norm, ROWS), jnp.ones(LANES - PIXELS, jnp.float32)])
    target = jnp.concatenate([jnp.asarray(place, jnp.float32), norm[None, :]], axis=0)
    row, col = np.divmod(np.arange(LANES), WIDE)
    source = jnp.asarray(np.stack([row, col - RIM_WIDTH], 1), jnp.float32)
    square = jax.ShapeDtypeStruct((DATE_ROWS, DATE_LANES), jnp.float32)
    weight = jax.ShapeDtypeStruct((LANES, LANES), jnp.bfloat16)
    return pl.pallas_call(
        operators_kernel,
        in_specs=[WHOLE] * 3,
        out_specs=[WHOLE] * 4,
        out_shape=[square] * 2 + [weight] * 2,
        scratch_shapes=[
            pltpu.VMEM((DATE_LANES, DATE_LANES), jnp.float32),
            pltpu.VMEM((DATE_LANES, 128), jnp.float32),
            pltpu.VMEM((DATE_ROWS, DATE_LANES), jnp.float32),
            pltpu.VMEM((DATE_ROWS, DATE_LANES), jnp.float32),
        ],
        compiler_params=pltpu.CompilerParams(vmem_limit_bytes=24 * MIB),
        cost_estimate=pl.CostEstimate(flops=20_000_000_000, bytes_accessed=3_000_000, transcendentals=0),
        name="operators",
    )(pairs, target, source)


def padded(value):
    return jnp.concatenate([value, jnp.zeros((DATE_LANES - DATE_ROWS, LANES), jnp.float32)], axis=0)


def gather_dates(ordered_ref, data_ref):
    def block(start):
        return split(data_ref[:, start : start + GROUP, :].reshape(GROUP * IFG_COUNT, 128))

    tails = [block(2 * OWN_IFGS), block(2 * OWN_IFGS + GROUP)]
    main, rest, spare = None, None, None
    for group in range(GROUPS):
        parts = [block(GROUP * group), block(OWN_IFGS + GROUP * group)]
        parts += tails if group == 2 else [tails[group]]
        design = one_hot(ordered_ref[:, 512 * group : 512 * group + 512], DATE_ROWS)
        high = jnp.concatenate([part[0] for part in parts], axis=1)
        low = jnp.concatenate([part[1] for part in parts], axis=1)
        sums = dot(design, high) + dot(design, low)
        main = sums[:, :256] if main is None else main + sums[:, :256]
        if group == 2:
            spare = sums[:, 256:]
        else:
            rest = sums[:, 256:] if rest is None else rest + sums[:, 256:]
    lane = iota((DATE_ROWS, 128), 1)
    first, second = shifted(spare[:, :128], 128 - TAIL), shifted(spare[:, 128:], 128 - TAIL + SPARE)
    rest = jnp.where(lane < TAIL, rest + jnp.where(lane < SPARE, first, second), 0.0)
    return jnp.concatenate([main, rest], axis=1)


def varying_kernel(ordered_ref, data_ref, filtered_ref, filter_high, filter_low, sums_ref, own_ref, top_ref, bottom_ref):
    sums = padded(gather_dates(ordered_ref, data_ref))
    sums_ref[...] = sums
    high, low = split(full_dot(filtered_ref[...], sums))
    smooth = dot(high, filter_high[...]) + (dot(high, filter_low[...]) + dot(low, filter_high[...]))
    smooth = padded(smooth).T
    own_ref[...] = smooth[:PIXELS]
    lane = iota((EDGE_PIXELS // 2, 128), 1)
    for edge_ref, first in ((top_ref, 0), (bottom_ref, PIXELS - EDGE_PIXELS)):
        edge = smooth[first : first + EDGE_PIXELS]
        edge_ref[0:EDGE_PIXELS, :] = edge[:, 0:128]
        edge_ref[EDGE_PIXELS : 2 * EDGE_PIXELS, :] = edge[:, 128:256]
        rest = edge[:, 256:]
        moved = pltpu.roll(rest[EDGE_PIXELS // 2 :], 64, 1)
        edge_ref[2 * EDGE_PIXELS :, :] = jnp.where(lane < 64, rest[: EDGE_PIXELS // 2], moved)


def project_varying(ordered, data, filtered, filter_high, filter_low):
    edge = jax.ShapeDtypeStruct((EDGE_ROWS, 128), jnp.float32)
    return pl.pallas_call(
        varying_kernel,
        in_specs=[WHOLE] * 5,
        out_specs=[WHOLE] * 4,
        out_shape=[
            jax.ShapeDtypeStruct((DATE_LANES, LANES), jnp.float32),
            jax.ShapeDtypeStruct((PIXELS, DATE_LANES), jnp.float32),
            edge,
            edge,
        ],
        compiler_params=pltpu.CompilerParams(vmem_limit_bytes=24 * MIB),
        cost_estimate=pl.CostEstimate(flops=1_100_000_000, bytes_accessed=5_000_000, transcendentals=0),
        name="varying",
    )(ordered, data, filtered, filter_high, filter_low)


def weight(offset):
    sigma = RIM_WIDTH / 2.0
    return float(np.exp(-offset * offset / (2.0 * sigma * sigma)))


def series_kernel(scale_ref, solve_ref, sums_ref, smooth_ref, series_ref, partial_ref):
    series = padded(full_dot(solve_ref[...], sums_ref[...])).T
    for row in range(ROWS):
        start = WIDE * row + RIM_WIDTH
        own = series[start : start + COLS]
        series_ref[row] = own[:, :DATES]
        total = None
        for other in range(ROWS):
            if abs(other - row) <= RIM_WIDTH:
                term = weight(other - row) * smooth_ref[COLS * other : COLS * (other + 1), :]
                total = term if total is None else total + term
        partial_ref[COLS * row : COLS * (row + 1), :] = own - total * scale_ref[row]


def project_series(row_scale, solve, sums, smooth):
    return pl.pallas_call(
        series_kernel,
        in_specs=[pl.BlockSpec(memory_space=pltpu.SMEM)] + [WHOLE] * 3,
        out_specs=[WHOLE] * 2,
        out_shape=[
            jax.ShapeDtypeStruct((ROWS, COLS, DATES), jnp.float32),
            jax.ShapeDtypeStruct((PIXELS, DATE_LANES), jnp.float32),
        ],
        compiler_params=pltpu.CompilerParams(vmem_limit_bytes=16 * MIB),
        cost_estimate=pl.CostEstimate(flops=2_000_000_000, bytes_accessed=2_000_000, transcendentals=0),
        name="series",
    )(row_scale, solve, sums, smooth)


def edge_tile(edge_ref, row, tile):
    if tile < 2:
        start = EDGE_PIXELS * tile + COLS * row
        return edge_ref[start : start + COLS, :]
    start = 2 * EDGE_PIXELS + COLS * (row % 2)
    return shifted(edge_ref[start : start + COLS, :], 64 * (row // 2))


def corrected_kernel(scale_ref, partial_ref, above_ref, below_ref, out_ref):
    for tile in range(3):
        above = [edge_tile(above_ref, row, tile) for row in range(RIM_WIDTH)]
        below = [edge_tile(below_ref, row, tile) for row in range(RIM_WIDTH)]
        for row in range(ROWS):
            near = [(other - RIM_WIDTH - row, above[other]) for other in range(RIM_WIDTH)]
            near += [(ROWS + other - row, below[other]) for other in range(RIM_WIDTH)]
            total = sum(weight(offset) * value for offset, value in near if abs(offset) <= RIM_WIDTH)
            part = partial_ref[COLS * row : COLS * (row + 1), 128 * tile : 128 * (tile + 1)]
            width = min(128, DATES - 128 * tile)
            out_ref[row, :, 128 * tile : 128 * tile + width] = (part - total * scale_ref[row])[:, :width]


def correct(row_scale, partial, above, below):
    return pl.pallas_call(
        corrected_kernel,
        in_specs=[pl.BlockSpec(memory_space=pltpu.SMEM)] + [WHOLE] * 3,
        out_specs=WHOLE,
        out_shape=jax.ShapeDtypeStruct((ROWS, COLS, DATES), jnp.float32),
        compiler_params=pltpu.CompilerParams(vmem_limit_bytes=16 * MIB),
        cost_estimate=pl.CostEstimate(flops=1_000_000, bytes_accessed=1_400_000, transcendentals=0),
        name="corrected",
    )(row_scale, partial, above, below)


def edge_weights(start, count, total):
    offsets = jnp.arange(-RIM_WIDTH, RIM_WIDTH + 1, dtype=jnp.int32)
    places = start + jnp.arange(count, dtype=jnp.int32)[:, None] + offsets[None, :]
    inside = ((places >= 0) & (places < total)).astype(jnp.float32)
    return jnp.sum(inside * tap(offsets.astype(jnp.float32))[None, :], axis=1)


def body(unwrapped, component_mask, date_pairs):
    blocks = pack(unwrapped.transpose(1, 0, 2), component_mask.transpose(1, 0, 2))
    data = lax.all_to_all(blocks, "ifg", split_axis=0, concat_axis=0, tiled=True)
    row_scale = 1.0 / edge_weights(lax.axis_index("band") * ROWS, ROWS, ROWS * BAND_COUNT)
    column_norm = edge_weights(lax.axis_index("ifg") * COLS, COLS, COLS * IFG_COUNT)
    pairs = date_pairs.T
    ordered = pairs.reshape(2, IFG_COUNT, GROUPS, GROUP).transpose(0, 2, 1, 3).reshape(2, IFGS)
    solve, filtered, filter_high, filter_low = operators(pairs, column_norm)
    sums, smooth, top, bottom = project_varying(ordered, data, filtered, filter_high, filter_low)
    down = [(i, i + 1) for i in range(BAND_COUNT - 1)]
    above = lax.ppermute(bottom, "band", down)
    below = lax.ppermute(top, "band", [(j, i) for i, j in down])
    series, partial = project_series(row_scale, solve, sums, smooth)
    corrected = correct(row_scale, partial, above, below)
    return series.transpose(2, 0, 1), corrected.transpose(2, 0, 1)


def solution(mesh):
    placed = (P("ifg", "band", None), P("ifg", "band", None), P())
    return jax.shard_map(
        body,
        mesh=mesh,
        in_specs=placed,
        out_specs=(P(None, "band", "ifg"), P(None, "band", "ifg")),
        check_vma=False,
    )
```

time: 110 us -> 91.5 us (0.83)
  the two profiles are of different devices: /device:TPU:70 before, /device:TPU:88 now
where the time goes in v2:
time: 91.5 us; the launch traced here: 91.2 us
  Pallas kernels  44.8 us (49%)
  waiting for transfers between devices  25.2 us (28%)
  starting transfers between devices  19 us (21%)
  local copies, waits for them, and re-layouts  1.14 us (1%)
    pallas_call x1, Pallas kernels, operators(): pl.pallas_call(operators_kernel, in_specs=[WHOLE] * 3, out_specs=[WHOLE]...  31.4 us
    all_to_all x1, waiting for transfers between devices, body(): lax.all_to_all(blocks, 'ifg', split_axis=0, concat_axis=0, tiled=True)  18.7 us
    all_to_all x1, starting transfers between devices, body(): lax.all_to_all(blocks, 'ifg', split_axis=0, concat_axis=0, tiled=True)  12.4 us
    pallas_call x1, Pallas kernels, pack(): pl.pallas_call(pack_kernel, grid=(steps,), in_specs=blocks + blocks, out_...  5.57 us
    ppermute x1, waiting for transfers between devices, body(): below = lax.ppermute(top, 'band', [(j, i) for i, j in down])  5.33 us
    ppermute x1, starting transfers between devices, body(): above = lax.ppermute(bottom, 'band', down)  4.69 us
    pallas_call x1, Pallas kernels, project_varying(): pl.pallas_call(varying_kernel, in_specs=[WHOLE] * 5, out_specs=[WHOLE] *...  3.84 us
    pallas_call x1, Pallas kernels, project_series(): pl.pallas_call(series_kernel, in_specs=[pl.BlockSpec(memory_space=pltpu.S...  2.57 us
  transfers between devices with their start and end apart: 3, of which 3 were waited for; matrix products, arithmetic and copies ran while one was open for 1% of the time, Pallas kernels for 37%

profile of v2, /device:TPU:88, one launch (start us, length us, event | category | flops | bytes accessed | tf_op | source)
XLA Modules:
  0.0 91.2 jit_solution(9086711068479034653)
XLA Ops:
  0.6 5.6 %mask_pack.1 = f32[32,128,128]{2,1,0:T(8,128)} custom-call(f32[6,48,1536]{2,1,0:T(8,128)} %bitcast.10, f32[6,48,1536]{2,1,0:T(8,128)} %bitcast.11, f32[6,48,1536]{2,1,0:T(8,128)} %bitcast.12, s32[6,48,1536]{2,1,0:T(8,128)} %bitcast.13, s32[6,48,1536]{2,1,0:T(8,128)} %bitcast.14, s32[6,48,1536]{2,1,0:T(8,128)} %bitcast.15), custom_call_target="tpu_custom_call" | custom-call | flops 2000000 | bytes 5600000 | tf_op jit(solution)/shard_map/mask_pack/pallas_call | solution.py:121
  6.2 0.0 copy-start
  6.2 0.0 copy-start.4
  6.2 0.0 copy-start.1
  6.2 12.4 %all-to-all-start = ((f32[32,128,128]{2,1,0:T(8,128)}), f32[32,128,128]{2,1,0:T(8,128)S(1)}, u32[]{:S(2)}, u32[]{:S(2)}) async-start(f32[32,128,128]{2,1,0:T(8,128)} %mask_pack.1), calls=%async_computation | async-start | bytes 4194304 | tf_op jit(solution)/shard_map/all_to_all | solution.py:381
  18.7 0.1 select_reduce_fusion
  18.8 0.1 tile.10
  18.9 0.0 copy-done
  18.9 0.1 reshape.35
  19.0 0.1 reshape.36.ordered_ref
  19.1 0.0 copy-done.4
  19.2 0.2 select_reduce_fusion.1
  19.4 0.0 copy-done.1
  19.4 31.4 %operators.1 = (f32[304,384]{1,0:T(8,128)S(1)}, f32[304,384]{1,0:T(8,128)S(1)}, bf16[384,384]{1,0:T(8,128)(2,1)S(1)}, bf16[384,384]{1,0:T(8,128)(2,1)S(1)}) custom-call(s32[2,1536]{1,0:T(2,128)S(1)} %bitcast.9, f32[3,384]{1,0:T(4,128)S(1)} %pad_maximum_fusion.target_ref, f32[384,2]{1,0:T(8,128)S(1)} %copy-done.1), custom_call_target="tpu_custom_call" | custom-call | flops 20000000000 | bytes 3000000 | tf_op jit(solution)/shard_map/operators/pallas_call | solution.py:225
  50.7 0.0 copy-start.2
  50.7 0.8 copy-done.2
  51.5 18.7 %all-to-all-done.data_ref = f32[32,128,128]{2,1,0:T(8,128)S(1)} async-done(((f32[32,128,128]{2,1,0:T(8,128)}), f32[32,128,128]{2,1,0:T(8,128)S(1)}, u32[]{:S(2)}, u32[]{:S(2)}) %all-to-all-start) | async-done | bytes 2097184 | tf_op jit(solution)/shard_map/all_to_all | solution.py:381
  70.2 0.0 copy-start.3
  70.2 3.8 %varying.1 = (f32[384,384]{1,0:T(8,128)S(1)}, f32[288,384]{1,0:T(8,128)S(1)}, f32[480,128]{1,0:T(8,128)S(1)}, f32[480,128]{1,0:T(8,128)S(1)}) custom-call(s32[2,1536]{1,0:T(2,128)S(1)} %reshape.36.ordered_ref, f32[32,128,128]{2,1,0:T(8,128)S(1)} %all-to-all-done.data_ref, f32[304,384]{1,0:T(8,128)S(1)} %get-tuple-element.13.filtered_ref, ...), custom_call_target="tpu_custom_call" | custom-call | flops 1100000000 | bytes 5000000 | tf_op jit(solution)/shard_map/varying/pallas_call | solution.py:289
  74.1 4.7 %collective-permute-start = (f32[480,128]{1,0:T(8,128)S(1)}, f32[480,128]{1,0:T(8,128)S(1)}, u32[]{:S(2)}, u32[]{:S(2)}) collective-permute-start(f32[480,128]{1,0:T(8,128)S(1)} %get-tuple-element.20), channel_id=1, source_target_pairs={{0,1},{1,2},{2,3},{3,4},{4,5},{5,6},{6,7},{7,8},{8,9},{9,10},{10,1... | collective-permute-start | bytes 737288 | tf_op jit(solution)/shard_map/ppermute | solution.py:389
  78.8 1.9 %collective-permute-start.1 = (f32[480,128]{1,0:T(8,128)S(1)}, f32[480,128]{1,0:T(8,128)S(1)}, u32[]{:S(2)}, u32[]{:S(2)}) collective-permute-start(f32[480,128]{1,0:T(8,128)S(1)} %get-tuple-element.21), channel_id=1, source_target_pairs={{1,0},{2,1},{3,2},{4,3},{5,4},{6,5},{7,6},{8,7},{9,8},{10,9},{11,1... | collective-permute-start | bytes 737288 | tf_op jit(solution)/shard_map/ppermute | solution.py:390
  80.7 0.0 copy-done.3
  80.7 2.6 %series.1 = (f32[6,48,300]{2,1,0:T(8,128)}, f32[288,384]{1,0:T(8,128)S(1)}) custom-call(f32[6]{0:T(128)S(1)} %broadcast_divide_fusion.scale_ref, f32[304,384]{1,0:T(8,128)S(1)} %copy-done.3, f32[384,384]{1,0:T(8,128)S(1)} %get-tuple-element.16.sums_ref, f32[288,384]{1,0:T(8,128)S(1)} %get-tuple-element.17.smooth_ref), custom_call_target="tpu_custom_call" | custom-call | flops 2000000000 | bytes 2000000 | tf_op jit(solution)/shard_map/series/pallas_call | solution.py:325
  83.3 1.2 %collective-permute-done.above_ref = f32[480,128]{1,0:T(8,128)S(1)} collective-permute-done((f32[480,128]{1,0:T(8,128)S(1)}, f32[480,128]{1,0:T(8,128)S(1)}, u32[]{:S(2)}, u32[]{:S(2)}) %collective-permute-start) | collective-permute-done | bytes 245792 | tf_op jit(solution)/shard_map/ppermute | solution.py:389
  84.5 5.3 %collective-permute-done.1.below_ref = f32[480,128]{1,0:T(8,128)S(1)} collective-permute-done((f32[480,128]{1,0:T(8,128)S(1)}, f32[480,128]{1,0:T(8,128)S(1)}, u32[]{:S(2)}, u32[]{:S(2)}) %collective-permute-start.1) | collective-permute-done | bytes 245792 | tf_op jit(solution)/shard_map/ppermute | solution.py:390
  89.8 1.4 %corrected.1 = f32[6,48,300]{2,1,0:T(8,128)} custom-call(f32[6]{0:T(128)S(1)} %broadcast_divide_fusion.scale_ref, f32[288,384]{1,0:T(8,128)S(1)} %get-tuple-element.19.partial_ref, f32[480,128]{1,0:T(8,128)S(1)} %collective-permute-done.above_ref, f32[480,128]{1,0:T(8,128)S(1)} %collective-permute-done.1.below_ref), custom_call_target="tpu_custom_call" | custom-call | flops 1000000 | bytes 1400000 | tf_op jit(solution)/shard_map/corrected/pallas_call | solution.py:361
  (10 shorter events, 0.1 us)
Async XLA Ops:
  6.2 12.7 %copy-start = (s32[1536,2]{0,1:T(2,128)S(1)}, s32[1536,2]{0,1:T(2,128)}, u32[]{:S(2)}) copy-start(s32[1536,2]{0,1:T(2,128)} %param.7) | copy-start | bytes 36868
  6.2 12.9 %copy-start.4 = (f32[2,384]{1,0:T(2,128)S(1)}, f32[2,384]{1,0:T(2,128)}, u32[]{:S(2)}) copy-start(f32[2,384]{1,0:T(2,128)} %constant.38.clone) | copy-start | bytes 9220
  6.2 13.1 %copy-start.1 = (f32[384,2]{1,0:T(8,128)S(1)}, f32[384,2]{1,0:T(8,128)}, u32[]{:S(2)}) copy-start(f32[384,2]{1,0:T(8,128)} %constant.39.clone.source_ref) | copy-start | bytes 9220
  6.2 64.0 %all-to-all-start = ((f32[32,128,128]{2,1,0:T(8,128)}), f32[32,128,128]{2,1,0:T(8,128)S(1)}, u32[]{:S(2)}, u32[]{:S(2)}) async-start(f32[32,128,128]{2,1,0:T(8,128)} %mask_pack.1), calls=%async_computation | async-start | bytes 4194304 | tf_op jit(solution)/shard_map/all_to_all | solution.py:381
  50.7 0.8 copy-start.2
  70.2 10.5 %copy-start.3 = (f32[304,384]{1,0:T(8,128)S(1)}, f32[304,384]{1,0:T(8,128)}, u32[]{:S(2)}) copy-start(f32[304,384]{1,0:T(8,128)} %copy-done.2) | copy-start | bytes 1400836
  74.1 10.4 %collective-permute-start = (f32[480,128]{1,0:T(8,128)S(1)}, f32[480,128]{1,0:T(8,128)S(1)}, u32[]{:S(2)}, u32[]{:S(2)}) collective-permute-start(f32[480,128]{1,0:T(8,128)S(1)} %get-tuple-element.20), channel_id=1, source_target_pairs={{0,1},{1,2},{2,3},{3,4},{4,5},{5,6},{6,7},{7,8},{8,9},{9,10},{10,1... | collective-permute-start | bytes 737288 | tf_op jit(solution)/shard_map/ppermute | solution.py:389
  78.8 11.0 %collective-permute-start.1 = (f32[480,128]{1,0:T(8,128)S(1)}, f32[480,128]{1,0:T(8,128)S(1)}, u32[]{:S(2)}, u32[]{:S(2)}) collective-permute-start(f32[480,128]{1,0:T(8,128)S(1)} %get-tuple-element.21), channel_id=1, source_target_pairs={{1,0},{2,1},{3,2},{4,3},{5,4},{6,5},{7,6},{8,7},{9,8},{10,9},{11,1... | collective-permute-start | bytes 737288 | tf_op jit(solution)/shard_map/ppermute | solution.py:390

commit v3 on v2

--- a/solution.py
+++ b/solution.py
@@ -31,9 +31,9 @@
 TAIL = WIDE_PIXELS - 256
 SPARE = 128 - TAIL
 BLOCK = 2 * OWN_IFGS + 2 * GROUP
-SEND_GROUP = 8
-SEND_COLS = SEND_GROUP * COLS
-SEND_TILES = SEND_COLS // 128
+CHUNKS = 4
+CHUNK = IFG_COUNT * COLS // CHUNKS
+STORE = 4
 
 EDGE_PIXELS = RIM_WIDTH * COLS
 EDGE_ROWS = 2 * EDGE_PIXELS + EDGE_PIXELS // 2
@@ -73,61 +73,89 @@
             yield source + start - pixel, base + start - first, stop - start
 
 
-def pack_kernel(*refs):
-    (before, inner, after), out_ref = zip(refs[0:3], refs[3:6]), refs[6]
-    step = pl.program_id(0)
-    lane = lax.broadcasted_iota(jnp.int32, (OWN_IFGS, 128), 1)
-    tail_lane = lax.broadcasted_iota(jnp.int32, (GROUP, 128), 1)
-
-    def masked(pair, row, tile):
-        at = (row, slice(None), slice(128 * tile, 128 * tile + 128))
-        return pair[0][at] * pair[1][at].astype(jnp.float32)
-
-    tiles = {}
+def needed_chunk(dest):
+    last = dest * COLS + COLS + RIM_WIDTH - 1
+    return min(last, IFG_COUNT * COLS - 1) // CHUNK
+
+
+def pack_kernel(unwrapped_ref, mask_ref, out_ref, phase, mask, masked, block, in_sem, out_sem):
+    loads = []
+    for chunk in range(CHUNKS):
+        at = (slice(None), slice(None), pl.ds(CHUNK * chunk, CHUNK))
+        pair = (
+            pltpu.make_async_copy(unwrapped_ref.at[at], phase.at[at], in_sem.at[0, chunk]),
+            pltpu.make_async_copy(mask_ref.at[at], mask.at[at], in_sem.at[1, chunk]),
+        )
+        for load in pair:
+            load.start()
+        loads.append(pair)
+    width = CHUNKS * CHUNK
     for row in range(ROWS):
-        tiles[row, -1] = jnp.where(step > 0, masked(before, row, 0), 0.0)
-        for tile in range(SEND_TILES):
-            tiles[row, tile] = masked(inner, row, tile)
-        tiles[row, SEND_TILES] = jnp.where(step < pl.num_programs(0) - 1, masked(after, row, 0), 0.0)
-    for dest in range(SEND_GROUP):
-        out = [jnp.zeros((OWN_IFGS, 128), jnp.float32) for _ in range(2)]
-        tail = [jnp.zeros((GROUP, 128), jnp.float32) for _ in range(2)]
+        masked[row, :, 0:128] = jnp.zeros((OWN_IFGS, 128), jnp.float32)
+        masked[row, :, 128 + width : 256 + width] = jnp.zeros((OWN_IFGS, 128), jnp.float32)
+    lane = lax.broadcasted_iota(jnp.int32, (GROUP, 128), 1)
+
+    def place(parts, rows, row, source, target, length):
+        for source_tile, tile, shift, first, last in pieces(source, target, length):
+            moved = shifted(masked[row, rows, 128 * source_tile : 128 * source_tile + 128], shift)
+            parts[tile] = jnp.where((lane >= first) & (lane < last), moved, parts[tile])
+
+    def fill(dest):
+        tail = [jnp.zeros((GROUP, 128), jnp.float32)] * 2
+        for group in range(GROUPS):
+            rows = slice(GROUP * group, GROUP * (group + 1))
+            main = [jnp.zeros((GROUP, 128), jnp.float32)] * 2
+            for row in range(ROWS):
+                source, target = 128 + dest * COLS - RIM_WIDTH, row * WIDE
+                length = min(max(256 - target, 0), WIDE)
+                place(main, rows, row, source, target, length)
+                for run in tail_runs(group, source + length, target + length - 256, WIDE - length):
+                    place(tail, rows, row, *run)
+            block[dest, rows, :] = main[0]
+            block[dest, OWN_IFGS + GROUP * group : OWN_IFGS + GROUP * (group + 1), :] = main[1]
+        block[dest, 2 * OWN_IFGS : 2 * OWN_IFGS + GROUP, :] = tail[0]
+        block[dest, 2 * OWN_IFGS + GROUP :, :] = tail[1]
+
+    stores = []
+    for chunk in range(CHUNKS):
+        for load in loads[chunk]:
+            load.wait()
         for row in range(ROWS):
-            source, target = dest * COLS - RIM_WIDTH, row * WIDE
-            length = min(max(256 - target, 0), WIDE)
-            for source_tile, tile, shift, first, last in pieces(source, target, length):
-                moved = shifted(tiles[row, source_tile], shift)
-                out[tile] = jnp.where((lane >= first) & (lane < last), moved, out[tile])
-            for group in range(GROUPS):
-                for run in tail_runs(group, source + length, target + length - 256, WIDE - length):
-                    for source_tile, tile, shift, first, last in pieces(*run):
-                        moved = shifted(tiles[row, source_tile][GROUP * group : GROUP * (group + 1)], shift)
-                        tail[tile] = jnp.where((tail_lane >= first) & (tail_lane < last), moved, tail[tile])
-        out_ref[dest, 0:OWN_IFGS, :] = out[0]
-        out_ref[dest, OWN_IFGS : 2 * OWN_IFGS, :] = out[1]
-        out_ref[dest, 2 * OWN_IFGS : 2 * OWN_IFGS + GROUP, :] = tail[0]
-        out_ref[dest, 2 * OWN_IFGS + GROUP :, :] = tail[1]
+            first = CHUNK * chunk
+            values = phase[row, :, first : first + CHUNK] * mask[row, :, first : first + CHUNK].astype(jnp.float32)
+            masked[row, :, 128 + first : 128 + first + CHUNK] = values
+        for dest in range(IFG_COUNT):
+            if needed_chunk(dest) == chunk:
+                fill(dest)
+                if (dest + 1) % STORE == 0:
+                    at = pl.ds(dest + 1 - STORE, STORE)
+                    store = pltpu.make_async_copy(block.at[at], out_ref.at[at], out_sem.at[dest // STORE])
+                    store.start()
+                    stores.append(store)
+    for store in stores:
+        store.wait()
 
 
 def pack(unwrapped, component_mask):
-    steps = IFG_COUNT // SEND_GROUP
-    last = SEND_TILES * steps - 1
-    tile = (ROWS, OWN_IFGS, 128)
-    blocks = [
-        pl.BlockSpec(tile, lambda i: (0, 0, jnp.maximum(SEND_TILES * i - 1, 0))),
-        pl.BlockSpec((ROWS, OWN_IFGS, SEND_COLS), lambda i: (0, 0, i)),
-        pl.BlockSpec(tile, lambda i: (0, 0, jnp.minimum(SEND_TILES * (i + 1), last))),
-    ]
+    anywhere = pl.BlockSpec(memory_space=pl.ANY)
+    columns = CHUNKS * CHUNK
     return pl.pallas_call(
         pack_kernel,
-        grid=(steps,),
-        in_specs=blocks + blocks,
-        out_specs=pl.BlockSpec((SEND_GROUP, BLOCK, 128), lambda i: (i, 0, 0)),
+        in_specs=[anywhere] * 2,
+        out_specs=anywhere,
         out_shape=jax.ShapeDtypeStruct((IFG_COUNT, BLOCK, 128), jnp.float32),
+        scratch_shapes=[
+            pltpu.VMEM((ROWS, OWN_IFGS, columns), jnp.float32),
+            pltpu.VMEM((ROWS, OWN_IFGS, columns), jnp.int32),
+            pltpu.VMEM((ROWS, OWN_IFGS, columns + 256), jnp.float32),
+            pltpu.VMEM((IFG_COUNT, BLOCK, 128), jnp.float32),
+            pltpu.SemaphoreType.DMA((2, CHUNKS)),
+            pltpu.SemaphoreType.DMA((IFG_COUNT // STORE,)),
+        ],
         compiler_params=pltpu.CompilerParams(vmem_limit_bytes=56 * MIB),
         cost_estimate=pl.CostEstimate(flops=2_000_000, bytes_accessed=5_600_000, transcendentals=0),
         name="mask_pack",
-    )(*[unwrapped] * 3, *[component_mask] * 3)
+    )(unwrapped, component_mask)
 
 
 def iota(shape, dim):
@@ -198,8 +226,14 @@
     return jnp.where(jnp.abs(offset) <= RIM_WIDTH, jnp.exp(-offset * offset / (2.0 * sigma * sigma)), 0.0)
 
 
-def operators_kernel(pairs_ref, target_ref, source_ref, solve_ref, filtered_ref, filter_high, filter_low,
-                     normal_ref, band_ref, lower_ref, scaled_ref):
+def split_three(value):
+    first = value.astype(jnp.bfloat16)
+    rest = value - first.astype(jnp.float32)
+    second = rest.astype(jnp.bfloat16)
+    return first, second, (rest - second.astype(jnp.float32)).astype(jnp.bfloat16)
+
+
+def operators_kernel(pairs_ref, solve_ref, first_ref, second_ref, third_ref, normal_ref, band_ref, lower_ref, scaled_ref):
     design = one_hot(pairs_ref[...], DATE_LANES)
     normal = lax.dot_general(design, design, (((1,), (1,)), ((), ())), preferred_element_type=jnp.float32)
     normal_ref[...] = normal + identity(DATE_LANES, DATE_LANES)
@@ -207,26 +241,16 @@
     solve = lax.dot_general(lower_ref[...], scaled_ref[...], (((0,), (0,)), ((), ())),
                             precision=lax.Precision.HIGHEST, preferred_element_type=jnp.float32)
     solve_ref[...] = solve[:DATE_ROWS]
-    filtered_ref[...] = full_dot(highpass_matrix(), solve)
-    same_row = source_ref[:, 0:1] == target_ref[0:1, :]
-    weights = tap(source_ref[:, 1:2] - target_ref[1:2, :]) / target_ref[2:3, :]
-    filter_high[...], filter_low[...] = split(jnp.where(same_row, weights, 0.0))
-
-
-def operators(pairs, column_norm):
-    row, col = np.divmod(np.arange(PIXELS), COLS)
-    place = np.stack([np.append(row, np.full(LANES - PIXELS, 2000)), np.append(col, np.zeros(LANES - PIXELS))])
-    norm = jnp.concatenate([jnp.tile(column_norm, ROWS), jnp.ones(LANES - PIXELS, jnp.float32)])
-    target = jnp.concatenate([jnp.asarray(place, jnp.float32), norm[None, :]], axis=0)
-    row, col = np.divmod(np.arange(LANES), WIDE)
-    source = jnp.asarray(np.stack([row, col - RIM_WIDTH], 1), jnp.float32)
-    square = jax.ShapeDtypeStruct((DATE_ROWS, DATE_LANES), jnp.float32)
-    weight = jax.ShapeDtypeStruct((LANES, LANES), jnp.bfloat16)
+    first_ref[...], second_ref[...], third_ref[...] = split_three(full_dot(highpass_matrix(), solve))
+
+
+def operators(pairs):
+    part = jax.ShapeDtypeStruct((DATE_ROWS, DATE_LANES), jnp.bfloat16)
     return pl.pallas_call(
         operators_kernel,
-        in_specs=[WHOLE] * 3,
+        in_specs=[WHOLE],
         out_specs=[WHOLE] * 4,
-        out_shape=[square] * 2 + [weight] * 2,
+        out_shape=[jax.ShapeDtypeStruct((DATE_ROWS, DATE_LANES), jnp.float32)] + [part] * 3,
         scratch_shapes=[
             pltpu.VMEM((DATE_LANES, DATE_LANES), jnp.float32),
             pltpu.VMEM((DATE_LANES, 128), jnp.float32),
@@ -236,7 +260,7 @@
         compiler_params=pltpu.CompilerParams(vmem_limit_bytes=24 * MIB),
         cost_estimate=pl.CostEstimate(flops=20_000_000_000, bytes_accessed=3_000_000, transcendentals=0),
         name="operators",
-    )(pairs, target, source)
+    )(pairs)
 
 
 def padded(value):
@@ -267,28 +291,53 @@
     return jnp.concatenate([main, rest], axis=1)
 
 
-def varying_kernel(ordered_ref, data_ref, filtered_ref, filter_high, filter_low, sums_ref, own_ref, top_ref, bottom_ref):
+def weight(offset):
+    sigma = RIM_WIDTH / 2.0
+    return float(np.exp(-offset * offset / (2.0 * sigma * sigma)))
+
+
+def varying_kernel(ordered_ref, data_ref, first_ref, second_ref, third_ref, scale_ref, sums_ref, own_ref, top_ref,
+                   bottom_ref, wide_ref):
     sums = padded(gather_dates(ordered_ref, data_ref))
     sums_ref[...] = sums
-    high, low = split(full_dot(filtered_ref[...], sums))
-    smooth = dot(high, filter_high[...]) + (dot(high, filter_low[...]) + dot(low, filter_high[...]))
-    smooth = padded(smooth).T
-    own_ref[...] = smooth[:PIXELS]
-    lane = iota((EDGE_PIXELS // 2, 128), 1)
-    for edge_ref, first in ((top_ref, 0), (bottom_ref, PIXELS - EDGE_PIXELS)):
-        edge = smooth[first : first + EDGE_PIXELS]
-        edge_ref[0:EDGE_PIXELS, :] = edge[:, 0:128]
-        edge_ref[EDGE_PIXELS : 2 * EDGE_PIXELS, :] = edge[:, 128:256]
-        rest = edge[:, 256:]
-        moved = pltpu.roll(rest[EDGE_PIXELS // 2 :], 64, 1)
-        edge_ref[2 * EDGE_PIXELS :, :] = jnp.where(lane < 64, rest[: EDGE_PIXELS // 2], moved)
-
-
-def project_varying(ordered, data, filtered, filter_high, filter_low):
+    left = [first_ref[...], second_ref[...], third_ref[...]]
+    right = split_three(sums)
+    orders = ((2, 0), (0, 2), (1, 1), (1, 0), (0, 1), (0, 0))
+    varying = dot(
+        jnp.concatenate([left[i] for i, _ in orders], axis=1), jnp.concatenate([right[j] for _, j in orders], axis=0)
+    )
+    varying = padded(varying).T
+    half = RIM_WIDTH // 2
+    lane = iota((COLS, 128), 1)
+    kept = {}
+    for tile in range(3):
+        wide_ref[tile] = varying[:, 128 * tile : 128 * (tile + 1)]
+        for row in range(ROWS):
+            start = WIDE * row + RIM_WIDTH
+            total = wide_ref[tile, start : start + COLS, :]
+            for offset in range(1, RIM_WIDTH + 1):
+                both = wide_ref[tile, start - offset : start - offset + COLS, :]
+                both = both + wide_ref[tile, start + offset : start + offset + COLS, :]
+                total = total + weight(offset) * both
+            total = total * scale_ref[...]
+            own_ref[COLS * row : COLS * (row + 1), 128 * tile : 128 * (tile + 1)] = total
+            for edge_ref, place in ((top_ref, row), (bottom_ref, row - (ROWS - RIM_WIDTH))):
+                if 0 <= place < RIM_WIDTH:
+                    if tile < 2:
+                        edge_ref[EDGE_PIXELS * tile + COLS * place : EDGE_PIXELS * tile + COLS * (place + 1), :] = total
+                    elif place < half:
+                        kept[row - place, place] = total
+                    else:
+                        start_row = 2 * EDGE_PIXELS + COLS * (place - half)
+                        packed = jnp.where(lane < 64, kept[row - place, place - half], pltpu.roll(total, 64, 1))
+                        edge_ref[start_row : start_row + COLS, :] = packed
+
+
+def project_varying(ordered, data, filtered, column_scale):
     edge = jax.ShapeDtypeStruct((EDGE_ROWS, 128), jnp.float32)
     return pl.pallas_call(
         varying_kernel,
-        in_specs=[WHOLE] * 5,
+        in_specs=[WHOLE] * 6,
         out_specs=[WHOLE] * 4,
         out_shape=[
             jax.ShapeDtypeStruct((DATE_LANES, LANES), jnp.float32),
@@ -296,15 +345,11 @@
             edge,
             edge,
         ],
+        scratch_shapes=[pltpu.VMEM((3, LANES, 128), jnp.float32)],
         compiler_params=pltpu.CompilerParams(vmem_limit_bytes=24 * MIB),
         cost_estimate=pl.CostEstimate(flops=1_100_000_000, bytes_accessed=5_000_000, transcendentals=0),
         name="varying",
-    )(ordered, data, filtered, filter_high, filter_low)
-
-
-def weight(offset):
-    sigma = RIM_WIDTH / 2.0
-    return float(np.exp(-offset * offset / (2.0 * sigma * sigma)))
+    )(ordered, data, *filtered, column_scale)
 
 
 def series_kernel(scale_ref, solve_ref, sums_ref, smooth_ref, series_ref, partial_ref):
@@ -344,25 +389,30 @@
     return shifted(edge_ref[start : start + COLS, :], 64 * (row // 2))
 
 
-def corrected_kernel(scale_ref, partial_ref, above_ref, below_ref, out_ref):
-    for tile in range(3):
-        above = [edge_tile(above_ref, row, tile) for row in range(RIM_WIDTH)]
-        below = [edge_tile(below_ref, row, tile) for row in range(RIM_WIDTH)]
-        for row in range(ROWS):
-            near = [(other - RIM_WIDTH - row, above[other]) for other in range(RIM_WIDTH)]
-            near += [(ROWS + other - row, below[other]) for other in range(RIM_WIDTH)]
-            total = sum(weight(offset) * value for offset, value in near if abs(offset) <= RIM_WIDTH)
+def corrected_kernel(scale_ref, partial_ref, above_ref, below_ref, out_ref, rows_ref, sem):
+    stores = []
+    for row in range(ROWS):
+        for tile in range(3):
+            near = [(other - RIM_WIDTH - row, above_ref, other) for other in range(RIM_WIDTH)]
+            near += [(ROWS + other - row, below_ref, other) for other in range(RIM_WIDTH)]
+            total = sum(weight(off) * edge_tile(ref, other, tile) for off, ref, other in near if abs(off) <= RIM_WIDTH)
             part = partial_ref[COLS * row : COLS * (row + 1), 128 * tile : 128 * (tile + 1)]
             width = min(128, DATES - 128 * tile)
-            out_ref[row, :, 128 * tile : 128 * tile + width] = (part - total * scale_ref[row])[:, :width]
+            rows_ref[row, :, 128 * tile : 128 * tile + width] = (part - total * scale_ref[row])[:, :width]
+        store = pltpu.make_async_copy(rows_ref.at[row], out_ref.at[row], sem.at[row])
+        store.start()
+        stores.append(store)
+    for store in stores:
+        store.wait()
 
 
 def correct(row_scale, partial, above, below):
     return pl.pallas_call(
         corrected_kernel,
         in_specs=[pl.BlockSpec(memory_space=pltpu.SMEM)] + [WHOLE] * 3,
-        out_specs=WHOLE,
+        out_specs=pl.BlockSpec(memory_space=pl.ANY),
         out_shape=jax.ShapeDtypeStruct((ROWS, COLS, DATES), jnp.float32),
+        scratch_shapes=[pltpu.VMEM((ROWS, COLS, DATES), jnp.float32), pltpu.SemaphoreType.DMA((ROWS,))],
         compiler_params=pltpu.CompilerParams(vmem_limit_bytes=16 * MIB),
         cost_estimate=pl.CostEstimate(flops=1_000_000, bytes_accessed=1_400_000, transcendentals=0),
         name="corrected",
@@ -383,8 +433,9 @@
     column_norm = edge_weights(lax.axis_index("ifg") * COLS, COLS, COLS * IFG_COUNT)
     pairs = date_pairs.T
     ordered = pairs.reshape(2, IFG_COUNT, GROUPS, GROUP).transpose(0, 2, 1, 3).reshape(2, IFGS)
-    solve, filtered, filter_high, filter_low = operators(pairs, column_norm)
-    sums, smooth, top, bottom = project_varying(ordered, data, filtered, filter_high, filter_low)
+    column_scale = jnp.broadcast_to((1.0 / column_norm)[:, None], (COLS, 128))
+    solve, *filtered = operators(pairs)
+    sums, smooth, top, bottom = project_varying(ordered, data, filtered, column_scale)
     down = [(i, i + 1) for i in range(BAND_COUNT - 1)]
     above = lax.ppermute(bottom, "band", down)
     below = lax.ppermute(top, "band", [(j, i) for i, j in down])

time: 91.5 us -> 88.5 us (0.967)
  Pallas kernels: 44.8 us -> 41.9 us
  waiting for transfers between devices: 25.2 us -> 26.2 us
    pallas_call x3, Pallas kernels: 40.8 us -> 37.9 us  [the longest x1 31.3 us: operators(): pl.pallas_call(operators_kernel, in_specs=[WHOLE], out_specs=[WHOLE] * 4,...]
    all_to_all x1, waiting for transfers between devices: 18.7 us -> 19.7 us  [body(): lax.all_to_all(blocks, 'ifg', split_axis=0, concat_axis=0, tiled=True)]
  transfers between devices with their start and end apart: 3 -> 3, of which waited for: 3 -> 3; matrix products, arithmetic and copies ran while one was open for 1% -> 1% of each run, Pallas kernels for 37% -> 38%
where the time goes in v3:
time: 88.5 us; the launch traced here: 88.3 us
  Pallas kernels  41.9 us (47%)
  waiting for transfers between devices  26.2 us (30%)
  starting transfers between devices  18.9 us (21%)
    pallas_call x1, Pallas kernels, operators(): pl.pallas_call(operators_kernel, in_specs=[WHOLE], out_specs=[WHOLE] * 4,...  31.3 us
    all_to_all x1, waiting for transfers between devices, body(): lax.all_to_all(blocks, 'ifg', split_axis=0, concat_axis=0, tiled=True)  19.7 us
    all_to_all x1, starting transfers between devices, body(): lax.all_to_all(blocks, 'ifg', split_axis=0, concat_axis=0, tiled=True)  12.3 us
    ppermute x1, waiting for transfers between devices, body(): below = lax.ppermute(top, 'band', [(j, i) for i, j in down])  5.33 us
    ppermute x1, starting transfers between devices, body(): above = lax.ppermute(bottom, 'band', down)  4.7 us
    pallas_call x1, Pallas kernels, pack(): pl.pallas_call(pack_kernel, in_specs=[anywhere] * 2, out_specs=anywhere,...  4.18 us
    pallas_call x1, Pallas kernels, project_series(): pl.pallas_call(series_kernel, in_specs=[pl.BlockSpec(memory_space=pltpu.S...  2.57 us
    pallas_call x1, Pallas kernels, project_varying(): pl.pallas_call(varying_kernel, in_specs=[WHOLE] * 6, out_specs=[WHOLE] *...  2.35 us
  transfers between devices with their start and end apart: 3, of which 3 were waited for; matrix products, arithmetic and copies ran while one was open for 1% of the time, Pallas kernels for 38%

profile of v3, /device:TPU:88, one launch (start us, length us, event | category | flops | bytes accessed | tf_op | source)
XLA Modules:
  0.0 88.3 jit_solution(16505993059915490818)
XLA Ops:
  0.6 4.2 %mask_pack.1 = f32[32,128,128]{2,1,0:T(8,128)} custom-call(f32[6,48,1536]{2,1,0:T(8,128)} %bitcast.10, s32[6,48,1536]{2,1,0:T(8,128)} %bitcast.11), custom_call_target="tpu_custom_call" | custom-call | flops 2000000 | bytes 5600000 | tf_op jit(solution)/shard_map/mask_pack/pallas_call | solution.py:142
  4.8 0.0 copy-start
  4.8 12.3 %all-to-all-start = ((f32[32,128,128]{2,1,0:T(8,128)}), f32[32,128,128]{2,1,0:T(8,128)S(1)}, u32[]{:S(2)}, u32[]{:S(2)}) async-start(f32[32,128,128]{2,1,0:T(8,128)} %mask_pack.1), calls=%async_computation | async-start | bytes 4194304 | tf_op jit(solution)/shard_map/all_to_all | solution.py:431
  17.1 0.0 copy-done
  17.1 0.1 reshape.37
  17.3 0.1 reshape.38.ordered_ref
  17.4 0.2 select_reduce_fusion.1
  17.6 0.1 select_reduce_fusion
  17.7 31.3 %operators.1 = (f32[304,384]{1,0:T(8,128)S(1)}, bf16[304,384]{1,0:T(8,128)(2,1)S(1)}, bf16[304,384]{1,0:T(8,128)(2,1)S(1)}, bf16[304,384]{1,0:T(8,128)(2,1)S(1)}) custom-call(s32[2,1536]{1,0:T(2,128)S(1)} %bitcast.9), custom_call_target="tpu_custom_call" | custom-call | flops 20000000000 | bytes 3000000 | tf_op jit(solution)/shard_map/operators/pallas_call | solution.py:249
  49.1 19.7 %all-to-all-done.data_ref = f32[32,128,128]{2,1,0:T(8,128)S(1)} async-done(((f32[32,128,128]{2,1,0:T(8,128)}), f32[32,128,128]{2,1,0:T(8,128)S(1)}, u32[]{:S(2)}, u32[]{:S(2)}) %all-to-all-start) | async-done | bytes 2097184 | tf_op jit(solution)/shard_map/all_to_all | solution.py:431
  68.7 0.1 broadcast_in_dim.8.scale_ref
  68.8 2.4 %varying.1 = (f32[384,384]{1,0:T(8,128)S(1)}, f32[288,384]{1,0:T(8,128)S(1)}, f32[480,128]{1,0:T(8,128)S(1)}, f32[480,128]{1,0:T(8,128)S(1)}) custom-call(s32[2,1536]{1,0:T(2,128)S(1)} %reshape.38.ordered_ref, f32[32,128,128]{2,1,0:T(8,128)S(1)} %all-to-all-done.data_ref, bf16[304,384]{1,0:T(8,128)(2,1)S(1)} %get-tuple-element.13.first_ref, ...), custom_call_target="tpu_custom_call" | custom-call | flops 1100000000 | bytes 5000000 | tf_op jit(solution)/shard_map/varying/pallas_call | solution.py:338
  71.1 4.7 %collective-permute-start = (f32[480,128]{1,0:T(8,128)S(1)}, f32[480,128]{1,0:T(8,128)S(1)}, u32[]{:S(2)}, u32[]{:S(2)}) collective-permute-start(f32[480,128]{1,0:T(8,128)S(1)} %get-tuple-element.20), channel_id=1, source_target_pairs={{0,1},{1,2},{2,3},{3,4},{4,5},{5,6},{6,7},{7,8},{8,9},{9,10},{10,1... | collective-permute-start | bytes 737288 | tf_op jit(solution)/shard_map/ppermute | solution.py:440
  75.9 1.9 %collective-permute-start.1 = (f32[480,128]{1,0:T(8,128)S(1)}, f32[480,128]{1,0:T(8,128)S(1)}, u32[]{:S(2)}, u32[]{:S(2)}) collective-permute-start(f32[480,128]{1,0:T(8,128)S(1)} %get-tuple-element.21), channel_id=1, source_target_pairs={{1,0},{2,1},{3,2},{4,3},{5,4},{6,5},{7,6},{8,7},{9,8},{10,9},{11,1... | collective-permute-start | bytes 737288 | tf_op jit(solution)/shard_map/ppermute | solution.py:441
  77.8 2.6 %series.1 = (f32[6,48,300]{2,1,0:T(8,128)}, f32[288,384]{1,0:T(8,128)S(1)}) custom-call(f32[6]{0:T(128)S(1)} %broadcast_divide_fusion.1.scale_ref, f32[304,384]{1,0:T(8,128)S(1)} %get-tuple-element.12.solve_ref, f32[384,384]{1,0:T(8,128)S(1)} %get-tuple-element.16.sums_ref, f32[288,384]{1,0:T(8,128)S(1)} %get-tuple-element.17.smooth_ref), custom_call_target="tpu_custom_call" | custom-call | flops 2000000000 | bytes 2000000 | tf_op jit(solution)/shard_map/series/pallas_call | solution.py:370
  80.4 1.2 %collective-permute-done.above_ref = f32[480,128]{1,0:T(8,128)S(1)} collective-permute-done((f32[480,128]{1,0:T(8,128)S(1)}, f32[480,128]{1,0:T(8,128)S(1)}, u32[]{:S(2)}, u32[]{:S(2)}) %collective-permute-start) | collective-permute-done | bytes 245792 | tf_op jit(solution)/shard_map/ppermute | solution.py:440
  81.5 5.3 %collective-permute-done.1.below_ref = f32[480,128]{1,0:T(8,128)S(1)} collective-permute-done((f32[480,128]{1,0:T(8,128)S(1)}, f32[480,128]{1,0:T(8,128)S(1)}, u32[]{:S(2)}, u32[]{:S(2)}) %collective-permute-start.1) | collective-permute-done | bytes 245792 | tf_op jit(solution)/shard_map/ppermute | solution.py:441
  86.9 1.4 %corrected.1 = f32[6,48,300]{2,1,0:T(8,128)} custom-call(f32[6]{0:T(128)S(1)} %broadcast_divide_fusion.1.scale_ref, f32[288,384]{1,0:T(8,128)S(1)} %get-tuple-element.19.partial_ref, f32[480,128]{1,0:T(8,128)S(1)} %collective-permute-done.above_ref, f32[480,128]{1,0:T(8,128)S(1)} %collective-permute-done.1.below_ref), custom_call_target="tpu_custom_call" | custom-call | flops 1000000 | bytes 1400000 | tf_op jit(solution)/shard_map/corrected/pallas_call | solution.py:410
  (7 shorter events, 0.0 us)
Async XLA Ops:
  4.8 12.3 %copy-start = (s32[1536,2]{0,1:T(2,128)S(1)}, s32[1536,2]{0,1:T(2,128)}, u32[]{:S(2)}) copy-start(s32[1536,2]{0,1:T(2,128)} %param.5) | copy-start | bytes 36868
  4.8 63.9 %all-to-all-start = ((f32[32,128,128]{2,1,0:T(8,128)}), f32[32,128,128]{2,1,0:T(8,128)S(1)}, u32[]{:S(2)}, u32[]{:S(2)}) async-start(f32[32,128,128]{2,1,0:T(8,128)} %mask_pack.1), calls=%async_computation | async-start | bytes 4194304 | tf_op jit(solution)/shard_map/all_to_all | solution.py:431
  71.1 10.4 %collective-permute-start = (f32[480,128]{1,0:T(8,128)S(1)}, f32[480,128]{1,0:T(8,128)S(1)}, u32[]{:S(2)}, u32[]{:S(2)}) collective-permute-start(f32[480,128]{1,0:T(8,128)S(1)} %get-tuple-element.20), channel_id=1, source_target_pairs={{0,1},{1,2},{2,3},{3,4},{4,5},{5,6},{6,7},{7,8},{8,9},{9,10},{10,1... | collective-permute-start | bytes 737288 | tf_op jit(solution)/shard_map/ppermute | solution.py:440
  75.9 11.0 %collective-permute-start.1 = (f32[480,128]{1,0:T(8,128)S(1)}, f32[480,128]{1,0:T(8,128)S(1)}, u32[]{:S(2)}, u32[]{:S(2)}) collective-permute-start(f32[480,128]{1,0:T(8,128)S(1)} %get-tuple-element.21), channel_id=1, source_target_pairs={{1,0},{2,1},{3,2},{4,3},{5,4},{6,5},{7,6},{8,7},{9,8},{10,9},{11,1... | collective-permute-start | bytes 737288 | tf_op jit(solution)/shard_map/ppermute | solution.py:441

commit v4 on v3

--- a/solution.py
+++ b/solution.py
@@ -39,6 +39,7 @@
 EDGE_ROWS = 2 * EDGE_PIXELS + EDGE_PIXELS // 2
 MIB = 1024 * 1024
 WHOLE = pl.BlockSpec(memory_space=pltpu.VMEM)
+SCALARS = pl.BlockSpec(memory_space=pltpu.SMEM)
 
 
 def split(value):
@@ -296,8 +297,25 @@
     return float(np.exp(-offset * offset / (2.0 * sigma * sigma)))
 
 
-def varying_kernel(ordered_ref, data_ref, first_ref, second_ref, third_ref, scale_ref, sums_ref, own_ref, top_ref,
-                   bottom_ref, wide_ref):
+def send_edge(edge_ref, own_ref, first):
+    half = RIM_WIDTH // 2
+    lane = iota((COLS, 128), 1)
+
+    def own(place, tile):
+        start = COLS * (first + place)
+        return own_ref[start : start + COLS, 128 * tile : 128 * (tile + 1)]
+
+    for place in range(RIM_WIDTH):
+        for tile in range(2):
+            start = EDGE_PIXELS * tile + COLS * place
+            edge_ref[start : start + COLS, :] = own(place, tile)
+    for place in range(half):
+        start = 2 * EDGE_PIXELS + COLS * place
+        edge_ref[start : start + COLS, :] = jnp.where(lane < 64, own(place, 2), pltpu.roll(own(place + half, 2), 64, 1))
+
+
+def varying_kernel(core_ref, ordered_ref, data_ref, first_ref, second_ref, third_ref, scale_ref, sums_ref, own_ref,
+                   edge_a_ref, edge_b_ref, wide_ref):
     sums = padded(gather_dates(ordered_ref, data_ref))
     sums_ref[...] = sums
     left = [first_ref[...], second_ref[...], third_ref[...]]
@@ -307,9 +325,6 @@
         jnp.concatenate([left[i] for i, _ in orders], axis=1), jnp.concatenate([right[j] for _, j in orders], axis=0)
     )
     varying = padded(varying).T
-    half = RIM_WIDTH // 2
-    lane = iota((COLS, 128), 1)
-    kept = {}
     for tile in range(3):
         wide_ref[tile] = varying[:, 128 * tile : 128 * (tile + 1)]
         for row in range(ROWS):
@@ -319,25 +334,20 @@
                 both = wide_ref[tile, start - offset : start - offset + COLS, :]
                 both = both + wide_ref[tile, start + offset : start + offset + COLS, :]
                 total = total + weight(offset) * both
-            total = total * scale_ref[...]
-            own_ref[COLS * row : COLS * (row + 1), 128 * tile : 128 * (tile + 1)] = total
-            for edge_ref, place in ((top_ref, row), (bottom_ref, row - (ROWS - RIM_WIDTH))):
-                if 0 <= place < RIM_WIDTH:
-                    if tile < 2:
-                        edge_ref[EDGE_PIXELS * tile + COLS * place : EDGE_PIXELS * tile + COLS * (place + 1), :] = total
-                    elif place < half:
-                        kept[row - place, place] = total
-                    else:
-                        start_row = 2 * EDGE_PIXELS + COLS * (place - half)
-                        packed = jnp.where(lane < 64, kept[row - place, place - half], pltpu.roll(total, 64, 1))
-                        edge_ref[start_row : start_row + COLS, :] = packed
-
-
-def project_varying(ordered, data, filtered, column_scale):
+            own_ref[COLS * row : COLS * (row + 1), 128 * tile : 128 * (tile + 1)] = total * scale_ref[...]
+    for core, (edge_down, edge_up) in enumerate(((edge_a_ref, edge_b_ref), (edge_b_ref, edge_a_ref))):
+
+        @pl.when(core_ref[0] == core)
+        def _():
+            send_edge(edge_down, own_ref, ROWS - RIM_WIDTH)
+            send_edge(edge_up, own_ref, 0)
+
+
+def project_varying(core, ordered, data, filtered, column_scale):
     edge = jax.ShapeDtypeStruct((EDGE_ROWS, 128), jnp.float32)
     return pl.pallas_call(
         varying_kernel,
-        in_specs=[WHOLE] * 6,
+        in_specs=[SCALARS] + [WHOLE] * 6,
         out_specs=[WHOLE] * 4,
         out_shape=[
             jax.ShapeDtypeStruct((DATE_LANES, LANES), jnp.float32),
@@ -349,7 +359,7 @@
         compiler_params=pltpu.CompilerParams(vmem_limit_bytes=24 * MIB),
         cost_estimate=pl.CostEstimate(flops=1_100_000_000, bytes_accessed=5_000_000, transcendentals=0),
         name="varying",
-    )(ordered, data, *filtered, column_scale)
+    )(core, ordered, data, *filtered, column_scale)
 
 
 def series_kernel(scale_ref, solve_ref, sums_ref, smooth_ref, series_ref, partial_ref):
@@ -369,7 +379,7 @@
 def project_series(row_scale, solve, sums, smooth):
     return pl.pallas_call(
         series_kernel,
-        in_specs=[pl.BlockSpec(memory_space=pltpu.SMEM)] + [WHOLE] * 3,
+        in_specs=[SCALARS] + [WHOLE] * 3,
         out_specs=[WHOLE] * 2,
         out_shape=[
             jax.ShapeDtypeStruct((ROWS, COLS, DATES), jnp.float32),
@@ -389,34 +399,42 @@
     return shifted(edge_ref[start : start + COLS, :], 64 * (row // 2))
 
 
-def corrected_kernel(scale_ref, partial_ref, above_ref, below_ref, out_ref, rows_ref, sem):
-    stores = []
-    for row in range(ROWS):
-        for tile in range(3):
-            near = [(other - RIM_WIDTH - row, above_ref, other) for other in range(RIM_WIDTH)]
-            near += [(ROWS + other - row, below_ref, other) for other in range(RIM_WIDTH)]
-            total = sum(weight(off) * edge_tile(ref, other, tile) for off, ref, other in near if abs(off) <= RIM_WIDTH)
-            part = partial_ref[COLS * row : COLS * (row + 1), 128 * tile : 128 * (tile + 1)]
-            width = min(128, DATES - 128 * tile)
-            rows_ref[row, :, 128 * tile : 128 * tile + width] = (part - total * scale_ref[row])[:, :width]
-        store = pltpu.make_async_copy(rows_ref.at[row], out_ref.at[row], sem.at[row])
-        store.start()
-        stores.append(store)
-    for store in stores:
-        store.wait()
-
-
-def correct(row_scale, partial, above, below):
+def corrected_kernel(core_ref, scale_ref, partial_ref, edge_a_ref, edge_b_ref, out_ref):
+    for core, (above_ref, below_ref) in enumerate(((edge_a_ref, edge_b_ref), (edge_b_ref, edge_a_ref))):
+
+        @pl.when(core_ref[0] == core)
+        def _():
+            for row in range(ROWS):
+                near = [(other - RIM_WIDTH - row, above_ref, other) for other in range(RIM_WIDTH)]
+                near += [(ROWS + other - row, below_ref, other) for other in range(RIM_WIDTH)]
+                near = [entry for entry in near if abs(entry[0]) <= RIM_WIDTH]
+                for tile in range(3):
+                    total = sum(weight(offset) * edge_tile(ref, other, tile) for offset, ref, other in near)
+                    part = partial_ref[COLS * row : COLS * (row + 1), 128 * tile : 128 * (tile + 1)]
+                    width = min(128, DATES - 128 * tile)
+                    out_ref[row, :, 128 * tile : 128 * tile + width] = (part - total * scale_ref[row])[:, :width]
+
+
+def correct(core, row_scale, partial, edge_a, edge_b):
     return pl.pallas_call(
         corrected_kernel,
-        in_specs=[pl.BlockSpec(memory_space=pltpu.SMEM)] + [WHOLE] * 3,
-        out_specs=pl.BlockSpec(memory_space=pl.ANY),
+        in_specs=[SCALARS] * 2 + [WHOLE] * 3,
+        out_specs=WHOLE,
         out_shape=jax.ShapeDtypeStruct((ROWS, COLS, DATES), jnp.float32),
-        scratch_shapes=[pltpu.VMEM((ROWS, COLS, DATES), jnp.float32), pltpu.SemaphoreType.DMA((ROWS,))],
         compiler_params=pltpu.CompilerParams(vmem_limit_bytes=16 * MIB),
         cost_estimate=pl.CostEstimate(flops=1_000_000, bytes_accessed=1_400_000, transcendentals=0),
         name="corrected",
-    )(row_scale, partial, above, below)
+    )(core, row_scale, partial, edge_a, edge_b)
+
+
+def pass_on(edge, first_way):
+    pairs = []
+    for i in range(IFG_COUNT):
+        way = first_way if i % 2 == 0 else -first_way
+        for b in range(BAND_COUNT):
+            if 0 <= b + way < BAND_COUNT:
+                pairs.append((i * BAND_COUNT + b, i * BAND_COUNT + b + way))
+    return lax.ppermute(edge, ("ifg", "band"), pairs)
 
 
 def edge_weights(start, count, total):
@@ -435,12 +453,11 @@
     ordered = pairs.reshape(2, IFG_COUNT, GROUPS, GROUP).transpose(0, 2, 1, 3).reshape(2, IFGS)
     column_scale = jnp.broadcast_to((1.0 / column_norm)[:, None], (COLS, 128))
     solve, *filtered = operators(pairs)
-    sums, smooth, top, bottom = project_varying(ordered, data, filtered, column_scale)
-    down = [(i, i + 1) for i in range(BAND_COUNT - 1)]
-    above = lax.ppermute(bottom, "band", down)
-    below = lax.ppermute(top, "band", [(j, i) for i, j in down])
+    core = (lax.axis_index("ifg") % 2)[None]
+    sums, smooth, edge_a, edge_b = project_varying(core, ordered, data, filtered, column_scale)
+    edge_a, edge_b = pass_on(edge_a, 1), pass_on(edge_b, -1)
     series, partial = project_series(row_scale, solve, sums, smooth)
-    corrected = correct(row_scale, partial, above, below)
+    corrected = correct(core, row_scale, partial, edge_a, edge_b)
     return series.transpose(2, 0, 1), corrected.transpose(2, 0, 1)
 
 

time: 88.5 us -> 86.9 us (0.982)
  waiting for transfers between devices: 26.2 us -> 24.4 us
    ppermute x2, waiting for transfers between devices: 6.5 us -> 4.78 us  [pass_on(): return lax.ppermute(edge, ('ifg', 'band'), pairs)]
  transfers between devices with their start and end apart: 3 -> 3, of which waited for: 3 -> 3; matrix products, arithmetic and copies ran while one was open for 1% -> 1% of each run, Pallas kernels for 38% -> 39%
where the time goes in v4:
time: 86.9 us; the launch traced here: 86.7 us
  Pallas kernels  41.9 us (48%)
  waiting for transfers between devices  24.4 us (28%)
  starting transfers between devices  18.9 us (22%)
    pallas_call x1, Pallas kernels, operators(): pl.pallas_call(operators_kernel, in_specs=[WHOLE], out_specs=[WHOLE] * 4,...  31.3 us
    all_to_all x1, waiting for transfers between devices, body(): lax.all_to_all(blocks, 'ifg', split_axis=0, concat_axis=0, tiled=True)  19.7 us
    all_to_all x1, starting transfers between devices, body(): lax.all_to_all(blocks, 'ifg', split_axis=0, concat_axis=0, tiled=True)  12.3 us
    ppermute x2, starting transfers between devices, pass_on(): return lax.ppermute(edge, ('ifg', 'band'), pairs)  6.62 us
    ppermute x2, waiting for transfers between devices, pass_on(): return lax.ppermute(edge, ('ifg', 'band'), pairs)  4.78 us
    pallas_call x1, Pallas kernels, pack(): pl.pallas_call(pack_kernel, in_specs=[anywhere] * 2, out_specs=anywhere,...  4.18 us
    pallas_call x1, Pallas kernels, project_series(): pl.pallas_call(series_kernel, in_specs=[SCALARS] + [WHOLE] * 3, out_specs...  2.58 us
    pallas_call x1, Pallas kernels, project_varying(): pl.pallas_call(varying_kernel, in_specs=[SCALARS] + [WHOLE] * 6, out_spec...  2.36 us
  transfers between devices with their start and end apart: 3, of which 3 were waited for; matrix products, arithmetic and copies ran while one was open for 1% of the time, Pallas kernels for 39%

profile of v4, /device:TPU:88, one launch (start us, length us, event | category | flops | bytes accessed | tf_op | source)
XLA Modules:
  0.0 86.7 jit_solution(6977561027723721005)
XLA Ops:
  0.6 4.2 %mask_pack.1 = f32[32,128,128]{2,1,0:T(8,128)} custom-call(f32[6,48,1536]{2,1,0:T(8,128)} %bitcast.11, s32[6,48,1536]{2,1,0:T(8,128)} %bitcast.12), custom_call_target="tpu_custom_call" | custom-call | flops 2000000 | bytes 5600000 | tf_op jit(solution)/shard_map/mask_pack/pallas_call | solution.py:143
  4.8 0.0 copy-start
  4.8 12.3 %all-to-all-start = ((f32[32,128,128]{2,1,0:T(8,128)}), f32[32,128,128]{2,1,0:T(8,128)S(1)}, u32[]{:S(2)}, u32[]{:S(2)}) async-start(f32[32,128,128]{2,1,0:T(8,128)} %mask_pack.1), calls=%async_computation | async-start | bytes 4194304 | tf_op jit(solution)/shard_map/all_to_all | solution.py:449
  17.1 0.0 copy-done
  17.1 0.1 reshape.37
  17.3 0.1 reshape.38.ordered_ref
  17.5 0.2 select_reduce_fusion.1
  17.6 0.1 select_reduce_fusion
  17.7 31.3 %operators.1 = (f32[304,384]{1,0:T(8,128)S(1)}, bf16[304,384]{1,0:T(8,128)(2,1)S(1)}, bf16[304,384]{1,0:T(8,128)(2,1)S(1)}, bf16[304,384]{1,0:T(8,128)(2,1)S(1)}) custom-call(s32[2,1536]{1,0:T(2,128)S(1)} %bitcast.10), custom_call_target="tpu_custom_call" | custom-call | flops 20000000000 | bytes 3000000 | tf_op jit(solution)/shard_map/operators/pallas_call | solution.py:250
  49.1 19.7 %all-to-all-done.data_ref = f32[32,128,128]{2,1,0:T(8,128)S(1)} async-done(((f32[32,128,128]{2,1,0:T(8,128)}), f32[32,128,128]{2,1,0:T(8,128)S(1)}, u32[]{:S(2)}, u32[]{:S(2)}) %all-to-all-start) | async-done | bytes 2097184 | tf_op jit(solution)/shard_map/all_to_all | solution.py:449
  68.7 0.1 broadcast_in_dim.11.scale_ref
  68.8 2.4 %varying.1 = (f32[384,384]{1,0:T(8,128)S(1)}, f32[288,384]{1,0:T(8,128)S(1)}, f32[480,128]{1,0:T(8,128)S(1)}, f32[480,128]{1,0:T(8,128)S(1)}) custom-call(s32[1]{0:T(128)} %bitcast.1.core_ref, s32[2,1536]{1,0:T(2,128)S(1)} %reshape.38.ordered_ref, f32[32,128,128]{2,1,0:T(8,128)S(1)} %all-to-all-done.data_ref, ...), custom_call_target="tpu_custom_call" | custom-call | flops 1100000000 | bytes 5000000 | tf_op jit(solution)/shard_map/varying/pallas_call | solution.py:348
  71.2 4.7 %collective-permute-start = (f32[480,128]{1,0:T(8,128)S(1)}, f32[480,128]{1,0:T(8,128)S(1)}, u32[]{:S(2)}, u32[]{:S(2)}) collective-permute-start(f32[480,128]{1,0:T(8,128)S(1)} %get-tuple-element.20), channel_id=1, source_target_pairs={{0,1},{1,2},{2,3},{3,4},{4,5},{5,6},{6,7},{7,8},{8,9},{9,10},{10,1... | collective-permute-start | bytes 737288 | tf_op jit(solution)/shard_map/ppermute | solution.py:437
  75.9 1.9 %collective-permute-start.1 = (f32[480,128]{1,0:T(8,128)S(1)}, f32[480,128]{1,0:T(8,128)S(1)}, u32[]{:S(2)}, u32[]{:S(2)}) collective-permute-start(f32[480,128]{1,0:T(8,128)S(1)} %get-tuple-element.21), channel_id=1, source_target_pairs={{1,0},{2,1},{3,2},{4,3},{5,4},{6,5},{7,6},{8,7},{9,8},{10,9},{11,1... | collective-permute-start | bytes 737288 | tf_op jit(solution)/shard_map/ppermute | solution.py:437
  77.8 2.6 %series.1 = (f32[6,48,300]{2,1,0:T(8,128)}, f32[288,384]{1,0:T(8,128)S(1)}) custom-call(f32[6]{0:T(128)S(1)} %broadcast_divide_fusion.1.scale_ref, f32[304,384]{1,0:T(8,128)S(1)} %get-tuple-element.12.solve_ref, f32[384,384]{1,0:T(8,128)S(1)} %get-tuple-element.16.sums_ref, f32[288,384]{1,0:T(8,128)S(1)} %get-tuple-element.17.smooth_ref), custom_call_target="tpu_custom_call" | custom-call | flops 2000000000 | bytes 2000000 | tf_op jit(solution)/shard_map/series/pallas_call | solution.py:380
  80.4 0.3 collective-permute-done.edge_a_ref
  80.7 4.5 %collective-permute-done.1.edge_b_ref = f32[480,128]{1,0:T(8,128)S(1)} collective-permute-done((f32[480,128]{1,0:T(8,128)S(1)}, f32[480,128]{1,0:T(8,128)S(1)}, u32[]{:S(2)}, u32[]{:S(2)}) %collective-permute-start.1) | collective-permute-done | bytes 245792 | tf_op jit(solution)/shard_map/ppermute | solution.py:437
  85.2 1.5 %corrected.1 = f32[6,48,300]{2,1,0:T(8,128)} custom-call(s32[1]{0:T(128)} %bitcast.1.core_ref, f32[6]{0:T(128)S(1)} %broadcast_divide_fusion.1.scale_ref, f32[288,384]{1,0:T(8,128)S(1)} %get-tuple-element.19.partial_ref, f32[480,128]{1,0:T(8,128)S(1)} %collective-permute-done.edge_a_ref, f32[480,128]{1,0:T(8,128)S(1)} %collective-permute-done.1.edge_b_ref), custom_call_target="tpu_custom_call" | custom-call | flops 1000000 | bytes 1400000 | tf_op jit(solution)/shard_map/corrected/pallas_call | solution.py:419
  (7 shorter events, 0.0 us)
Async XLA Ops:
  4.8 12.3 %copy-start = (s32[1536,2]{0,1:T(2,128)S(1)}, s32[1536,2]{0,1:T(2,128)}, u32[]{:S(2)}) copy-start(s32[1536,2]{0,1:T(2,128)} %param.5) | copy-start | bytes 36868
  4.8 63.9 %all-to-all-start = ((f32[32,128,128]{2,1,0:T(8,128)}), f32[32,128,128]{2,1,0:T(8,128)S(1)}, u32[]{:S(2)}, u32[]{:S(2)}) async-start(f32[32,128,128]{2,1,0:T(8,128)} %mask_pack.1), calls=%async_computation | async-start | bytes 4194304 | tf_op jit(solution)/shard_map/all_to_all | solution.py:449
  71.2 9.5 %collective-permute-start = (f32[480,128]{1,0:T(8,128)S(1)}, f32[480,128]{1,0:T(8,128)S(1)}, u32[]{:S(2)}, u32[]{:S(2)}) collective-permute-start(f32[480,128]{1,0:T(8,128)S(1)} %get-tuple-element.20), channel_id=1, source_target_pairs={{0,1},{1,2},{2,3},{3,4},{4,5},{5,6},{6,7},{7,8},{8,9},{9,10},{10,1... | collective-permute-start | bytes 737288 | tf_op jit(solution)/shard_map/ppermute | solution.py:437
  75.9 9.3 %collective-permute-start.1 = (f32[480,128]{1,0:T(8,128)S(1)}, f32[480,128]{1,0:T(8,128)S(1)}, u32[]{:S(2)}, u32[]{:S(2)}) collective-permute-start(f32[480,128]{1,0:T(8,128)S(1)} %get-tuple-element.21), channel_id=1, source_target_pairs={{1,0},{2,1},{3,2},{4,3},{5,4},{6,5},{7,6},{8,7},{9,8},{10,9},{11,1... | collective-permute-start | bytes 737288 | tf_op jit(solution)/shard_map/ppermute | solution.py:437

commit v5 on v4

--- a/solution.py
+++ b/solution.py
@@ -39,7 +39,6 @@
 EDGE_ROWS = 2 * EDGE_PIXELS + EDGE_PIXELS // 2
 MIB = 1024 * 1024
 WHOLE = pl.BlockSpec(memory_space=pltpu.VMEM)
-SCALARS = pl.BlockSpec(memory_space=pltpu.SMEM)
 
 
 def split(value):
@@ -314,7 +313,7 @@
         edge_ref[start : start + COLS, :] = jnp.where(lane < 64, own(place, 2), pltpu.roll(own(place + half, 2), 64, 1))
 
 
-def varying_kernel(core_ref, ordered_ref, data_ref, first_ref, second_ref, third_ref, scale_ref, sums_ref, own_ref,
+def varying_kernel(ordered_ref, data_ref, first_ref, second_ref, third_ref, scale_ref, sums_ref, own_ref,
                    edge_a_ref, edge_b_ref, wide_ref):
     sums = padded(gather_dates(ordered_ref, data_ref))
     sums_ref[...] = sums
@@ -337,17 +336,17 @@
             own_ref[COLS * row : COLS * (row + 1), 128 * tile : 128 * (tile + 1)] = total * scale_ref[...]
     for core, (edge_down, edge_up) in enumerate(((edge_a_ref, edge_b_ref), (edge_b_ref, edge_a_ref))):
 
-        @pl.when(core_ref[0] == core)
+        @pl.when(lax.axis_index("ifg") % 2 == core)
         def _():
             send_edge(edge_down, own_ref, ROWS - RIM_WIDTH)
             send_edge(edge_up, own_ref, 0)
 
 
-def project_varying(core, ordered, data, filtered, column_scale):
+def project_varying(ordered, data, filtered, column_scale):
     edge = jax.ShapeDtypeStruct((EDGE_ROWS, 128), jnp.float32)
     return pl.pallas_call(
         varying_kernel,
-        in_specs=[SCALARS] + [WHOLE] * 6,
+        in_specs=[WHOLE] * 6,
         out_specs=[WHOLE] * 4,
         out_shape=[
             jax.ShapeDtypeStruct((DATE_LANES, LANES), jnp.float32),
@@ -359,7 +358,7 @@
         compiler_params=pltpu.CompilerParams(vmem_limit_bytes=24 * MIB),
         cost_estimate=pl.CostEstimate(flops=1_100_000_000, bytes_accessed=5_000_000, transcendentals=0),
         name="varying",
-    )(core, ordered, data, *filtered, column_scale)
+    )(ordered, data, *filtered, column_scale)
 
 
 def series_kernel(scale_ref, solve_ref, sums_ref, smooth_ref, series_ref, partial_ref):
@@ -373,13 +372,13 @@
             if abs(other - row) <= RIM_WIDTH:
                 term = weight(other - row) * smooth_ref[COLS * other : COLS * (other + 1), :]
                 total = term if total is None else total + term
-        partial_ref[COLS * row : COLS * (row + 1), :] = own - total * scale_ref[row]
+        partial_ref[COLS * row : COLS * (row + 1), :] = own - total * jnp.concatenate([scale_ref[row : row + 1, :]] * 3, axis=1)
 
 
 def project_series(row_scale, solve, sums, smooth):
     return pl.pallas_call(
         series_kernel,
-        in_specs=[SCALARS] + [WHOLE] * 3,
+        in_specs=[WHOLE] * 4,
         out_specs=[WHOLE] * 2,
         out_shape=[
             jax.ShapeDtypeStruct((ROWS, COLS, DATES), jnp.float32),
@@ -399,32 +398,33 @@
     return shifted(edge_ref[start : start + COLS, :], 64 * (row // 2))
 
 
-def corrected_kernel(core_ref, scale_ref, partial_ref, edge_a_ref, edge_b_ref, out_ref):
+def corrected_kernel(scale_ref, partial_ref, edge_a_ref, edge_b_ref, out_ref):
     for core, (above_ref, below_ref) in enumerate(((edge_a_ref, edge_b_ref), (edge_b_ref, edge_a_ref))):
 
-        @pl.when(core_ref[0] == core)
+        @pl.when(lax.axis_index("ifg") % 2 == core)
         def _():
             for row in range(ROWS):
                 near = [(other - RIM_WIDTH - row, above_ref, other) for other in range(RIM_WIDTH)]
                 near += [(ROWS + other - row, below_ref, other) for other in range(RIM_WIDTH)]
                 near = [entry for entry in near if abs(entry[0]) <= RIM_WIDTH]
+                scale = scale_ref[row : row + 1, :]
                 for tile in range(3):
                     total = sum(weight(offset) * edge_tile(ref, other, tile) for offset, ref, other in near)
                     part = partial_ref[COLS * row : COLS * (row + 1), 128 * tile : 128 * (tile + 1)]
                     width = min(128, DATES - 128 * tile)
-                    out_ref[row, :, 128 * tile : 128 * tile + width] = (part - total * scale_ref[row])[:, :width]
-
-
-def correct(core, row_scale, partial, edge_a, edge_b):
+                    out_ref[row, :, 128 * tile : 128 * tile + width] = (part - total * scale)[:, :width]
+
+
+def correct(row_scale, partial, edge_a, edge_b):
     return pl.pallas_call(
         corrected_kernel,
-        in_specs=[SCALARS] * 2 + [WHOLE] * 3,
+        in_specs=[WHOLE] * 4,
         out_specs=WHOLE,
         out_shape=jax.ShapeDtypeStruct((ROWS, COLS, DATES), jnp.float32),
         compiler_params=pltpu.CompilerParams(vmem_limit_bytes=16 * MIB),
         cost_estimate=pl.CostEstimate(flops=1_000_000, bytes_accessed=1_400_000, transcendentals=0),
         name="corrected",
-    )(core, row_scale, partial, edge_a, edge_b)
+    )(row_scale, partial, edge_a, edge_b)
 
 
 def pass_on(edge, first_way):
@@ -447,17 +447,17 @@
 def body(unwrapped, component_mask, date_pairs):
     blocks = pack(unwrapped.transpose(1, 0, 2), component_mask.transpose(1, 0, 2))
     data = lax.all_to_all(blocks, "ifg", split_axis=0, concat_axis=0, tiled=True)
-    row_scale = 1.0 / edge_weights(lax.axis_index("band") * ROWS, ROWS, ROWS * BAND_COUNT)
+    row_norm = edge_weights(lax.axis_index("band") * ROWS, ROWS, ROWS * BAND_COUNT)
+    row_scale = jnp.broadcast_to((1.0 / row_norm)[:, None], (ROWS, 128))
     column_norm = edge_weights(lax.axis_index("ifg") * COLS, COLS, COLS * IFG_COUNT)
     pairs = date_pairs.T
     ordered = pairs.reshape(2, IFG_COUNT, GROUPS, GROUP).transpose(0, 2, 1, 3).reshape(2, IFGS)
     column_scale = jnp.broadcast_to((1.0 / column_norm)[:, None], (COLS, 128))
     solve, *filtered = operators(pairs)
-    core = (lax.axis_index("ifg") % 2)[None]
-    sums, smooth, edge_a, edge_b = project_varying(core, ordered, data, filtered, column_scale)
+    sums, smooth, edge_a, edge_b = project_varying(ordered, data, filtered, column_scale)
     edge_a, edge_b = pass_on(edge_a, 1), pass_on(edge_b, -1)
     series, partial = project_series(row_scale, solve, sums, smooth)
-    corrected = correct(core, row_scale, partial, edge_a, edge_b)
+    corrected = correct(row_scale, partial, edge_a, edge_b)
     return series.transpose(2, 0, 1), corrected.transpose(2, 0, 1)
 
 

time: 86.9 us -> 86.3 us (level)
  Pallas kernels: 41.9 us -> 40.8 us
    pallas_call x3, Pallas kernels: 6.43 us -> 5.27 us  [the longest x1 2.34 us: project_varying(): pl.pallas_call(varying_kernel, in_specs=[WHOLE] * 6, out_specs=[WHOLE] *...]
where the time goes in v5:
time: 86.3 us; the launch traced here: 86.1 us
  Pallas kernels  40.8 us (47%)
  waiting for transfers between devices  24.9 us (29%)
  starting transfers between devices  18.9 us (22%)
    pallas_call x1, Pallas kernels, operators(): pl.pallas_call(operators_kernel, in_specs=[WHOLE], out_specs=[WHOLE] * 4,...  31.3 us
    all_to_all x1, waiting for transfers between devices, body(): lax.all_to_all(blocks, 'ifg', split_axis=0, concat_axis=0, tiled=True)  19.7 us
    all_to_all x1, starting transfers between devices, body(): lax.all_to_all(blocks, 'ifg', split_axis=0, concat_axis=0, tiled=True)  12.3 us
    ppermute x2, starting transfers between devices, pass_on(): return lax.ppermute(edge, ('ifg', 'band'), pairs)  6.62 us
    ppermute x2, waiting for transfers between devices, pass_on(): return lax.ppermute(edge, ('ifg', 'band'), pairs)  5.26 us
    pallas_call x1, Pallas kernels, pack(): pl.pallas_call(pack_kernel, in_specs=[anywhere] * 2, out_specs=anywhere,...  4.18 us
    pallas_call x1, Pallas kernels, project_varying(): pl.pallas_call(varying_kernel, in_specs=[WHOLE] * 6, out_specs=[WHOLE] *...  2.34 us
    pallas_call x1, Pallas kernels, project_series(): pl.pallas_call(series_kernel, in_specs=[WHOLE] * 4, out_specs=[WHOLE] * 2...  2.02 us
  transfers between devices with their start and end apart: 3, of which 3 were waited for; matrix products, arithmetic and copies ran while one was open for 1% of the time, Pallas kernels for 39%

profile of v5, /device:TPU:88, one launch (start us, length us, event | category | flops | bytes accessed | tf_op | source)
XLA Modules:
  0.0 86.1 jit_solution(4548469177743581189)
XLA Ops:
  0.6 4.2 %mask_pack.1 = f32[32,128,128]{2,1,0:T(8,128)} custom-call(f32[6,48,1536]{2,1,0:T(8,128)} %bitcast.10, s32[6,48,1536]{2,1,0:T(8,128)} %bitcast.11), custom_call_target="tpu_custom_call" | custom-call | flops 2000000 | bytes 5600000 | tf_op jit(solution)/shard_map/mask_pack/pallas_call | solution.py:142
  4.8 0.0 copy-start
  4.8 12.3 %all-to-all-start = ((f32[32,128,128]{2,1,0:T(8,128)}), f32[32,128,128]{2,1,0:T(8,128)S(1)}, u32[]{:S(2)}, u32[]{:S(2)}) async-start(f32[32,128,128]{2,1,0:T(8,128)} %mask_pack.1), calls=%async_computation | async-start | bytes 4194304 | tf_op jit(solution)/shard_map/all_to_all | solution.py:449
  17.1 0.0 copy-done
  17.1 0.1 reshape.40
  17.3 0.1 reshape.41.ordered_ref
  17.4 0.2 select_reduce_fusion.1
  17.6 0.1 select_reduce_fusion
  17.7 31.3 %operators.1 = (f32[304,384]{1,0:T(8,128)S(1)}, bf16[304,384]{1,0:T(8,128)(2,1)S(1)}, bf16[304,384]{1,0:T(8,128)(2,1)S(1)}, bf16[304,384]{1,0:T(8,128)(2,1)S(1)}) custom-call(s32[2,1536]{1,0:T(2,128)S(1)} %bitcast.9), custom_call_target="tpu_custom_call" | custom-call | flops 20000000000 | bytes 3000000 | tf_op jit(solution)/shard_map/operators/pallas_call | solution.py:249
  49.1 19.7 %all-to-all-done.data_ref = f32[32,128,128]{2,1,0:T(8,128)S(1)} async-done(((f32[32,128,128]{2,1,0:T(8,128)}), f32[32,128,128]{2,1,0:T(8,128)S(1)}, u32[]{:S(2)}, u32[]{:S(2)}) %all-to-all-start) | async-done | bytes 2097184 | tf_op jit(solution)/shard_map/all_to_all | solution.py:449
  68.7 0.1 broadcast_in_dim.11.scale_ref
  68.8 2.3 %varying.1 = (f32[384,384]{1,0:T(8,128)S(1)}, f32[288,384]{1,0:T(8,128)S(1)}, f32[480,128]{1,0:T(8,128)S(1)}, f32[480,128]{1,0:T(8,128)S(1)}) custom-call(s32[2,1536]{1,0:T(2,128)S(1)} %reshape.41.ordered_ref, f32[32,128,128]{2,1,0:T(8,128)S(1)} %all-to-all-done.data_ref, bf16[304,384]{1,0:T(8,128)(2,1)S(1)} %get-tuple-element.13.first_ref, ...), custom_call_target="tpu_custom_call" | custom-call | flops 1100000000 | bytes 5000000 | tf_op jit(solution)/shard_map/varying/pallas_call | solution.py:347
  71.1 4.7 %collective-permute-start = (f32[480,128]{1,0:T(8,128)S(1)}, f32[480,128]{1,0:T(8,128)S(1)}, u32[]{:S(2)}, u32[]{:S(2)}) collective-permute-start(f32[480,128]{1,0:T(8,128)S(1)} %get-tuple-element.20), channel_id=1, source_target_pairs={{0,1},{1,2},{2,3},{3,4},{4,5},{5,6},{6,7},{7,8},{8,9},{9,10},{10,1... | collective-permute-start | bytes 737288 | tf_op jit(solution)/shard_map/ppermute | solution.py:437
  75.8 1.9 %collective-permute-start.1 = (f32[480,128]{1,0:T(8,128)S(1)}, f32[480,128]{1,0:T(8,128)S(1)}, u32[]{:S(2)}, u32[]{:S(2)}) collective-permute-start(f32[480,128]{1,0:T(8,128)S(1)} %get-tuple-element.21), channel_id=1, source_target_pairs={{1,0},{2,1},{3,2},{4,3},{5,4},{6,5},{7,6},{8,7},{9,8},{10,9},{11,1... | collective-permute-start | bytes 737288 | tf_op jit(solution)/shard_map/ppermute | solution.py:437
  77.8 0.1 broadcast_in_dim.10.scale_ref
  77.9 2.0 %series.1 = (f32[6,48,300]{2,1,0:T(8,128)}, f32[288,384]{1,0:T(8,128)S(1)}) custom-call(f32[6,128]{1,0:T(8,128)S(1)} %broadcast_in_dim.10.scale_ref, f32[304,384]{1,0:T(8,128)S(1)} %get-tuple-element.12.solve_ref, f32[384,384]{1,0:T(8,128)S(1)} %get-tuple-element.16.sums_ref, f32[288,384]{1,0:T(8,128)S(1)} %get-tuple-element.17.smooth_ref), custom_call_target="tpu_custom_call" | custom-call | flops 2000000000 | bytes 2000000 | tf_op jit(solution)/shard_map/series/pallas_call | solution.py:379
  79.9 0.8 collective-permute-done.edge_a_ref
  80.7 4.5 %collective-permute-done.1.edge_b_ref = f32[480,128]{1,0:T(8,128)S(1)} collective-permute-done((f32[480,128]{1,0:T(8,128)S(1)}, f32[480,128]{1,0:T(8,128)S(1)}, u32[]{:S(2)}, u32[]{:S(2)}) %collective-permute-start.1) | collective-permute-done | bytes 245792 | tf_op jit(solution)/shard_map/ppermute | solution.py:437
  85.1 0.9 %corrected.1 = f32[6,48,300]{2,1,0:T(8,128)} custom-call(f32[6,128]{1,0:T(8,128)S(1)} %broadcast_in_dim.10.scale_ref, f32[288,384]{1,0:T(8,128)S(1)} %get-tuple-element.19.partial_ref, f32[480,128]{1,0:T(8,128)S(1)} %collective-permute-done.edge_a_ref, f32[480,128]{1,0:T(8,128)S(1)} %collective-permute-done.1.edge_b_ref), custom_call_target="tpu_custom_call" | custom-call | flops 1000000 | bytes 1400000 | tf_op jit(solution)/shard_map/corrected/pallas_call | solution.py:419
  (7 shorter events, 0.0 us)
Async XLA Ops:
  4.8 12.3 %copy-start = (s32[1536,2]{0,1:T(2,128)S(1)}, s32[1536,2]{0,1:T(2,128)}, u32[]{:S(2)}) copy-start(s32[1536,2]{0,1:T(2,128)} %param.5) | copy-start | bytes 36868
  4.8 63.9 %all-to-all-start = ((f32[32,128,128]{2,1,0:T(8,128)}), f32[32,128,128]{2,1,0:T(8,128)S(1)}, u32[]{:S(2)}, u32[]{:S(2)}) async-start(f32[32,128,128]{2,1,0:T(8,128)} %mask_pack.1), calls=%async_computation | async-start | bytes 4194304 | tf_op jit(solution)/shard_map/all_to_all | solution.py:449
  71.1 9.5 %collective-permute-start = (f32[480,128]{1,0:T(8,128)S(1)}, f32[480,128]{1,0:T(8,128)S(1)}, u32[]{:S(2)}, u32[]{:S(2)}) collective-permute-start(f32[480,128]{1,0:T(8,128)S(1)} %get-tuple-element.20), channel_id=1, source_target_pairs={{0,1},{1,2},{2,3},{3,4},{4,5},{5,6},{6,7},{7,8},{8,9},{9,10},{10,1... | collective-permute-start | bytes 737288 | tf_op jit(solution)/shard_map/ppermute | solution.py:437
  75.8 9.3 %collective-permute-start.1 = (f32[480,128]{1,0:T(8,128)S(1)}, f32[480,128]{1,0:T(8,128)S(1)}, u32[]{:S(2)}, u32[]{:S(2)}) collective-permute-start(f32[480,128]{1,0:T(8,128)S(1)} %get-tuple-element.21), channel_id=1, source_target_pairs={{1,0},{2,1},{3,2},{4,3},{5,4},{6,5},{7,6},{8,7},{9,8},{10,9},{11,1... | collective-permute-start | bytes 737288 | tf_op jit(solution)/shard_map/ppermute | solution.py:437

commit v6 on v5

--- a/solution.py
+++ b/solution.py
@@ -55,22 +55,8 @@
     return jnp.dot(a, b, precision=lax.Precision.HIGHEST, preferred_element_type=jnp.float32)
 
 
-def pieces(source, target, length):
-    while length > 0:
-        step = min(length, 128 - source % 128, 128 - target % 128)
-        yield source // 128, target // 128, (target - source) % 128, target % 128, target % 128 + step
-        source, target, length = source + step, target + step, length - step
-
-
 def shifted(value, shift):
     return value if shift == 0 else pltpu.roll(value, shift, 1)
-
-
-def tail_runs(group, source, pixel, length):
-    for first, last, base in ((0, TAIL, 128 * group),) if group < 2 else ((0, SPARE, TAIL), (SPARE, TAIL, 128 + TAIL)):
-        start, stop = max(pixel, first), min(pixel + length, last)
-        if start < stop:
-            yield source + start - pixel, base + start - first, stop - start
 
 
 def needed_chunk(dest):
@@ -95,22 +81,36 @@
         masked[row, :, 128 + width : 256 + width] = jnp.zeros((OWN_IFGS, 128), jnp.float32)
     lane = lax.broadcasted_iota(jnp.int32, (GROUP, 128), 1)
 
-    def place(parts, rows, row, source, target, length):
-        for source_tile, tile, shift, first, last in pieces(source, target, length):
-            moved = shifted(masked[row, rows, 128 * source_tile : 128 * source_tile + 128], shift)
-            parts[tile] = jnp.where((lane >= first) & (lane < last), moved, parts[tile])
-
     def fill(dest):
-        tail = [jnp.zeros((GROUP, 128), jnp.float32)] * 2
+        source_tile, start = divmod(128 + dest * COLS - RIM_WIDTH, 128)
+        tail = [None] * 2
         for group in range(GROUPS):
             rows = slice(GROUP * group, GROUP * (group + 1))
-            main = [jnp.zeros((GROUP, 128), jnp.float32)] * 2
+            main = [None] * 2
+
+            def put(parts, tile, first, moved):
+                parts[tile] = moved if first == 0 else jnp.where(lane >= first, moved, parts[tile])
+
             for row in range(ROWS):
-                source, target = 128 + dest * COLS - RIM_WIDTH, row * WIDE
-                length = min(max(256 - target, 0), WIDE)
-                place(main, rows, row, source, target, length)
-                for run in tail_runs(group, source + length, target + length - 256, WIDE - length):
-                    place(tail, rows, row, *run)
+                run = masked[row, rows, 128 * source_tile : 128 * source_tile + 128]
+                if start + WIDE > 128:
+                    rest = masked[row, rows, 128 * source_tile + 128 : 128 * source_tile + 256]
+                    run = jnp.where(lane >= start, run, rest)
+                target = row * WIDE
+                moved = shifted(run, (target - start) % 128)
+                tile, first = divmod(target, 128)
+                if tile < 2:
+                    put(main, tile, first, moved)
+                    if tile == 0 and first + WIDE > 128:
+                        put(main, 1, 0, moved)
+                beyond = max(target - 256, 0)
+                if target + WIDE > 256 and group < 2:
+                    put(tail, group, beyond, moved)
+                elif target + WIDE > 256:
+                    if beyond < SPARE:
+                        put(tail, 0, TAIL + beyond, shifted(run, (target - start + TAIL) % 128))
+                    if target + WIDE - 256 > SPARE:
+                        put(tail, 1, TAIL + max(beyond - SPARE, 0), shifted(run, (target - start + TAIL - SPARE) % 128))
             block[dest, rows, :] = main[0]
             block[dest, OWN_IFGS + GROUP * group : OWN_IFGS + GROUP * (group + 1), :] = main[1]
         block[dest, 2 * OWN_IFGS : 2 * OWN_IFGS + GROUP, :] = tail[0]

time: 86.3 us -> 85.7 us (level)
  no operation moved by 1% of the time
where the time goes in v6:
time: 85.7 us; the launch traced here: 85.5 us
  Pallas kernels  40.2 us (47%)
  waiting for transfers between devices  24.9 us (29%)
  starting transfers between devices  18.9 us (22%)
    pallas_call x1, Pallas kernels, operators(): pl.pallas_call(operators_kernel, in_specs=[WHOLE], out_specs=[WHOLE] * 4,...  31.3 us
    all_to_all x1, waiting for transfers between devices, body(): lax.all_to_all(blocks, 'ifg', split_axis=0, concat_axis=0, tiled=True)  19.7 us
    all_to_all x1, starting transfers between devices, body(): lax.all_to_all(blocks, 'ifg', split_axis=0, concat_axis=0, tiled=True)  12.3 us
    ppermute x2, starting transfers between devices, pass_on(): return lax.ppermute(edge, ('ifg', 'band'), pairs)  6.62 us
    ppermute x2, waiting for transfers between devices, pass_on(): return lax.ppermute(edge, ('ifg', 'band'), pairs)  5.26 us
    pallas_call x1, Pallas kernels, pack(): pl.pallas_call(pack_kernel, in_specs=[anywhere] * 2, out_specs=anywhere,...  3.62 us
    pallas_call x1, Pallas kernels, project_varying(): pl.pallas_call(varying_kernel, in_specs=[WHOLE] * 6, out_specs=[WHOLE] *...  2.34 us
    pallas_call x1, Pallas kernels, project_series(): pl.pallas_call(series_kernel, in_specs=[WHOLE] * 4, out_specs=[WHOLE] * 2...  2.02 us
  transfers between devices with their start and end apart: 3, of which 3 were waited for; matrix products, arithmetic and copies ran while one was open for 1% of the time, Pallas kernels for 39%

profile of v6, /device:TPU:88, one launch (start us, length us, event | category | flops | bytes accessed | tf_op | source)
XLA Modules:
  0.0 85.5 jit_solution(17333019120205044533)
XLA Ops:
  0.6 3.6 %mask_pack.1 = f32[32,128,128]{2,1,0:T(8,128)} custom-call(f32[6,48,1536]{2,1,0:T(8,128)} %bitcast.10, s32[6,48,1536]{2,1,0:T(8,128)} %bitcast.11), custom_call_target="tpu_custom_call" | custom-call | flops 2000000 | bytes 5600000 | tf_op jit(solution)/shard_map/mask_pack/pallas_call | solution.py:142
  4.3 0.0 copy-start
  4.3 12.3 %all-to-all-start = ((f32[32,128,128]{2,1,0:T(8,128)}), f32[32,128,128]{2,1,0:T(8,128)S(1)}, u32[]{:S(2)}, u32[]{:S(2)}) async-start(f32[32,128,128]{2,1,0:T(8,128)} %mask_pack.1), calls=%async_computation | async-start | bytes 4194304 | tf_op jit(solution)/shard_map/all_to_all | solution.py:449
  16.6 0.0 copy-done
  16.6 0.1 reshape.40
  16.7 0.1 reshape.41.ordered_ref
  16.9 0.2 select_reduce_fusion.1
  17.1 0.1 select_reduce_fusion
  17.2 31.3 %operators.1 = (f32[304,384]{1,0:T(8,128)S(1)}, bf16[304,384]{1,0:T(8,128)(2,1)S(1)}, bf16[304,384]{1,0:T(8,128)(2,1)S(1)}, bf16[304,384]{1,0:T(8,128)(2,1)S(1)}) custom-call(s32[2,1536]{1,0:T(2,128)S(1)} %bitcast.9), custom_call_target="tpu_custom_call" | custom-call | flops 20000000000 | bytes 3000000 | tf_op jit(solution)/shard_map/operators/pallas_call | solution.py:249
  48.5 19.7 %all-to-all-done.data_ref = f32[32,128,128]{2,1,0:T(8,128)S(1)} async-done(((f32[32,128,128]{2,1,0:T(8,128)}), f32[32,128,128]{2,1,0:T(8,128)S(1)}, u32[]{:S(2)}, u32[]{:S(2)}) %all-to-all-start) | async-done | bytes 2097184 | tf_op jit(solution)/shard_map/all_to_all | solution.py:449
  68.2 0.1 broadcast_in_dim.11.scale_ref
  68.2 2.3 %varying.1 = (f32[384,384]{1,0:T(8,128)S(1)}, f32[288,384]{1,0:T(8,128)S(1)}, f32[480,128]{1,0:T(8,128)S(1)}, f32[480,128]{1,0:T(8,128)S(1)}) custom-call(s32[2,1536]{1,0:T(2,128)S(1)} %reshape.41.ordered_ref, f32[32,128,128]{2,1,0:T(8,128)S(1)} %all-to-all-done.data_ref, bf16[304,384]{1,0:T(8,128)(2,1)S(1)} %get-tuple-element.13.first_ref, ...), custom_call_target="tpu_custom_call" | custom-call | flops 1100000000 | bytes 5000000 | tf_op jit(solution)/shard_map/varying/pallas_call | solution.py:347
  70.6 4.7 %collective-permute-start = (f32[480,128]{1,0:T(8,128)S(1)}, f32[480,128]{1,0:T(8,128)S(1)}, u32[]{:S(2)}, u32[]{:S(2)}) collective-permute-start(f32[480,128]{1,0:T(8,128)S(1)} %get-tuple-element.20), channel_id=1, source_target_pairs={{0,1},{1,2},{2,3},{3,4},{4,5},{5,6},{6,7},{7,8},{8,9},{9,10},{10,1... | collective-permute-start | bytes 737288 | tf_op jit(solution)/shard_map/ppermute | solution.py:437
  75.3 1.9 %collective-permute-start.1 = (f32[480,128]{1,0:T(8,128)S(1)}, f32[480,128]{1,0:T(8,128)S(1)}, u32[]{:S(2)}, u32[]{:S(2)}) collective-permute-start(f32[480,128]{1,0:T(8,128)S(1)} %get-tuple-element.21), channel_id=1, source_target_pairs={{1,0},{2,1},{3,2},{4,3},{5,4},{6,5},{7,6},{8,7},{9,8},{10,9},{11,1... | collective-permute-start | bytes 737288 | tf_op jit(solution)/shard_map/ppermute | solution.py:437
  77.2 0.1 broadcast_in_dim.10.scale_ref
  77.3 2.0 %series.1 = (f32[6,48,300]{2,1,0:T(8,128)}, f32[288,384]{1,0:T(8,128)S(1)}) custom-call(f32[6,128]{1,0:T(8,128)S(1)} %broadcast_in_dim.10.scale_ref, f32[304,384]{1,0:T(8,128)S(1)} %get-tuple-element.12.solve_ref, f32[384,384]{1,0:T(8,128)S(1)} %get-tuple-element.16.sums_ref, f32[288,384]{1,0:T(8,128)S(1)} %get-tuple-element.17.smooth_ref), custom_call_target="tpu_custom_call" | custom-call | flops 2000000000 | bytes 2000000 | tf_op jit(solution)/shard_map/series/pallas_call | solution.py:379
  79.3 0.8 collective-permute-done.edge_a_ref
  80.1 4.5 %collective-permute-done.1.edge_b_ref = f32[480,128]{1,0:T(8,128)S(1)} collective-permute-done((f32[480,128]{1,0:T(8,128)S(1)}, f32[480,128]{1,0:T(8,128)S(1)}, u32[]{:S(2)}, u32[]{:S(2)}) %collective-permute-start.1) | collective-permute-done | bytes 245792 | tf_op jit(solution)/shard_map/ppermute | solution.py:437
  84.6 0.9 %corrected.1 = f32[6,48,300]{2,1,0:T(8,128)} custom-call(f32[6,128]{1,0:T(8,128)S(1)} %broadcast_in_dim.10.scale_ref, f32[288,384]{1,0:T(8,128)S(1)} %get-tuple-element.19.partial_ref, f32[480,128]{1,0:T(8,128)S(1)} %collective-permute-done.edge_a_ref, f32[480,128]{1,0:T(8,128)S(1)} %collective-permute-done.1.edge_b_ref), custom_call_target="tpu_custom_call" | custom-call | flops 1000000 | bytes 1400000 | tf_op jit(solution)/shard_map/corrected/pallas_call | solution.py:419
  (7 shorter events, 0.0 us)
Async XLA Ops:
  4.3 12.3 %copy-start = (s32[1536,2]{0,1:T(2,128)S(1)}, s32[1536,2]{0,1:T(2,128)}, u32[]{:S(2)}) copy-start(s32[1536,2]{0,1:T(2,128)} %param.5) | copy-start | bytes 36868
  4.3 63.9 %all-to-all-start = ((f32[32,128,128]{2,1,0:T(8,128)}), f32[32,128,128]{2,1,0:T(8,128)S(1)}, u32[]{:S(2)}, u32[]{:S(2)}) async-start(f32[32,128,128]{2,1,0:T(8,128)} %mask_pack.1), calls=%async_computation | async-start | bytes 4194304 | tf_op jit(solution)/shard_map/all_to_all | solution.py:449
  70.6 9.5 %collective-permute-start = (f32[480,128]{1,0:T(8,128)S(1)}, f32[480,128]{1,0:T(8,128)S(1)}, u32[]{:S(2)}, u32[]{:S(2)}) collective-permute-start(f32[480,128]{1,0:T(8,128)S(1)} %get-tuple-element.20), channel_id=1, source_target_pairs={{0,1},{1,2},{2,3},{3,4},{4,5},{5,6},{6,7},{7,8},{8,9},{9,10},{10,1... | collective-permute-start | bytes 737288 | tf_op jit(solution)/shard_map/ppermute | solution.py:437
  75.3 9.3 %collective-permute-start.1 = (f32[480,128]{1,0:T(8,128)S(1)}, f32[480,128]{1,0:T(8,128)S(1)}, u32[]{:S(2)}, u32[]{:S(2)}) collective-permute-start(f32[480,128]{1,0:T(8,128)S(1)} %get-tuple-element.21), channel_id=1, source_target_pairs={{1,0},{2,1},{3,2},{4,3},{5,4},{6,5},{7,6},{8,7},{9,8},{10,9},{11,1... | collective-permute-start | bytes 737288 | tf_op jit(solution)/shard_map/ppermute | solution.py:437

commit v7 on v6

--- a/solution.py
+++ b/solution.py
@@ -122,7 +122,8 @@
             load.wait()
         for row in range(ROWS):
             first = CHUNK * chunk
-            values = phase[row, :, first : first + CHUNK] * mask[row, :, first : first + CHUNK].astype(jnp.float32)
+            inside = mask[row, :, first : first + CHUNK] != 0
+            values = jnp.where(inside, phase[row, :, first : first + CHUNK], 0.0)
             masked[row, :, 128 + first : 128 + first + CHUNK] = values
         for dest in range(IFG_COUNT):
             if needed_chunk(dest) == chunk:
@@ -164,8 +165,8 @@
 
 def one_hot(pairs, dates):
     date = iota((dates, pairs.shape[1]), 0)
-    later = jnp.where(pairs[1:2, :] == date, 1.0, 0.0)
-    return (later - jnp.where(pairs[0:1, :] == date, 1.0, 0.0)).astype(jnp.bfloat16)
+    earlier = jnp.where(pairs[0:1, :] == date, -1.0, 0.0)
+    return jnp.where(pairs[1:2, :] == date, 1.0, earlier).astype(jnp.bfloat16)
 
 
 def identity(rows, cols, first=0):

time: 85.7 us -> 85.7 us (level)
  no operation moved by 1% of the time
where the time goes in v7:
time: 85.7 us; the launch traced here: 85.5 us
  Pallas kernels  40.2 us (47%)
  waiting for transfers between devices  25 us (29%)
  starting transfers between devices  18.9 us (22%)
    pallas_call x1, Pallas kernels, operators(): pl.pallas_call(operators_kernel, in_specs=[WHOLE], out_specs=[WHOLE] * 4,...  31.3 us
    all_to_all x1, waiting for transfers between devices, body(): lax.all_to_all(blocks, 'ifg', split_axis=0, concat_axis=0, tiled=True)  19.7 us
    all_to_all x1, starting transfers between devices, body(): lax.all_to_all(blocks, 'ifg', split_axis=0, concat_axis=0, tiled=True)  12.3 us
    ppermute x2, starting transfers between devices, pass_on(): return lax.ppermute(edge, ('ifg', 'band'), pairs)  6.62 us
    ppermute x2, waiting for transfers between devices, pass_on(): return lax.ppermute(edge, ('ifg', 'band'), pairs)  5.27 us
    pallas_call x1, Pallas kernels, pack(): pl.pallas_call(pack_kernel, in_specs=[anywhere] * 2, out_specs=anywhere,...  3.62 us
    pallas_call x1, Pallas kernels, project_varying(): pl.pallas_call(varying_kernel, in_specs=[WHOLE] * 6, out_specs=[WHOLE] *...  2.34 us
    pallas_call x1, Pallas kernels, project_series(): pl.pallas_call(series_kernel, in_specs=[WHOLE] * 4, out_specs=[WHOLE] * 2...  2.02 us
  transfers between devices with their start and end apart: 3, of which 3 were waited for; matrix products, arithmetic and copies ran while one was open for 1% of the time, Pallas kernels for 39%

profile of v7, /device:TPU:88, one launch (start us, length us, event | category | flops | bytes accessed | tf_op | source)
XLA Modules:
  0.0 85.5 jit_solution(8202394642017482285)
XLA Ops:
  0.6 3.6 %mask_pack.1 = f32[32,128,128]{2,1,0:T(8,128)} custom-call(f32[6,48,1536]{2,1,0:T(8,128)} %bitcast.10, s32[6,48,1536]{2,1,0:T(8,128)} %bitcast.11), custom_call_target="tpu_custom_call" | custom-call | flops 2000000 | bytes 5600000 | tf_op jit(solution)/shard_map/mask_pack/pallas_call | solution.py:143
  4.3 0.0 copy-start
  4.3 12.3 %all-to-all-start = ((f32[32,128,128]{2,1,0:T(8,128)}), f32[32,128,128]{2,1,0:T(8,128)S(1)}, u32[]{:S(2)}, u32[]{:S(2)}) async-start(f32[32,128,128]{2,1,0:T(8,128)} %mask_pack.1), calls=%async_computation | async-start | bytes 4194304 | tf_op jit(solution)/shard_map/all_to_all | solution.py:450
  16.5 0.0 copy-done
  16.6 0.1 reshape.40
  16.7 0.1 reshape.41.ordered_ref
  16.9 0.2 select_reduce_fusion.1
  17.1 0.1 select_reduce_fusion
  17.2 31.3 %operators.1 = (f32[304,384]{1,0:T(8,128)S(1)}, bf16[304,384]{1,0:T(8,128)(2,1)S(1)}, bf16[304,384]{1,0:T(8,128)(2,1)S(1)}, bf16[304,384]{1,0:T(8,128)(2,1)S(1)}) custom-call(s32[2,1536]{1,0:T(2,128)S(1)} %bitcast.9), custom_call_target="tpu_custom_call" | custom-call | flops 20000000000 | bytes 3000000 | tf_op jit(solution)/shard_map/operators/pallas_call | solution.py:250
  48.5 19.7 %all-to-all-done.data_ref = f32[32,128,128]{2,1,0:T(8,128)S(1)} async-done(((f32[32,128,128]{2,1,0:T(8,128)}), f32[32,128,128]{2,1,0:T(8,128)S(1)}, u32[]{:S(2)}, u32[]{:S(2)}) %all-to-all-start) | async-done | bytes 2097184 | tf_op jit(solution)/shard_map/all_to_all | solution.py:450
  68.2 0.1 broadcast_in_dim.11.scale_ref
  68.2 2.3 %varying.1 = (f32[384,384]{1,0:T(8,128)S(1)}, f32[288,384]{1,0:T(8,128)S(1)}, f32[480,128]{1,0:T(8,128)S(1)}, f32[480,128]{1,0:T(8,128)S(1)}) custom-call(s32[2,1536]{1,0:T(2,128)S(1)} %reshape.41.ordered_ref, f32[32,128,128]{2,1,0:T(8,128)S(1)} %all-to-all-done.data_ref, bf16[304,384]{1,0:T(8,128)(2,1)S(1)} %get-tuple-element.13.first_ref, ...), custom_call_target="tpu_custom_call" | custom-call | flops 1100000000 | bytes 5000000 | tf_op jit(solution)/shard_map/varying/pallas_call | solution.py:348
  70.6 4.7 %collective-permute-start = (f32[480,128]{1,0:T(8,128)S(1)}, f32[480,128]{1,0:T(8,128)S(1)}, u32[]{:S(2)}, u32[]{:S(2)}) collective-permute-start(f32[480,128]{1,0:T(8,128)S(1)} %get-tuple-element.20), channel_id=1, source_target_pairs={{0,1},{1,2},{2,3},{3,4},{4,5},{5,6},{6,7},{7,8},{8,9},{9,10},{10,1... | collective-permute-start | bytes 737288 | tf_op jit(solution)/shard_map/ppermute | solution.py:438
  75.3 1.9 %collective-permute-start.1 = (f32[480,128]{1,0:T(8,128)S(1)}, f32[480,128]{1,0:T(8,128)S(1)}, u32[]{:S(2)}, u32[]{:S(2)}) collective-permute-start(f32[480,128]{1,0:T(8,128)S(1)} %get-tuple-element.21), channel_id=1, source_target_pairs={{1,0},{2,1},{3,2},{4,3},{5,4},{6,5},{7,6},{8,7},{9,8},{10,9},{11,1... | collective-permute-start | bytes 737288 | tf_op jit(solution)/shard_map/ppermute | solution.py:438
  77.2 0.1 broadcast_in_dim.10.scale_ref
  77.3 2.0 %series.1 = (f32[6,48,300]{2,1,0:T(8,128)}, f32[288,384]{1,0:T(8,128)S(1)}) custom-call(f32[6,128]{1,0:T(8,128)S(1)} %broadcast_in_dim.10.scale_ref, f32[304,384]{1,0:T(8,128)S(1)} %get-tuple-element.12.solve_ref, f32[384,384]{1,0:T(8,128)S(1)} %get-tuple-element.16.sums_ref, f32[288,384]{1,0:T(8,128)S(1)} %get-tuple-element.17.smooth_ref), custom_call_target="tpu_custom_call" | custom-call | flops 2000000000 | bytes 2000000 | tf_op jit(solution)/shard_map/series/pallas_call | solution.py:380
  79.3 0.8 collective-permute-done.edge_a_ref
  80.1 4.5 %collective-permute-done.1.edge_b_ref = f32[480,128]{1,0:T(8,128)S(1)} collective-permute-done((f32[480,128]{1,0:T(8,128)S(1)}, f32[480,128]{1,0:T(8,128)S(1)}, u32[]{:S(2)}, u32[]{:S(2)}) %collective-permute-start.1) | collective-permute-done | bytes 245792 | tf_op jit(solution)/shard_map/ppermute | solution.py:438
  84.6 0.9 %corrected.1 = f32[6,48,300]{2,1,0:T(8,128)} custom-call(f32[6,128]{1,0:T(8,128)S(1)} %broadcast_in_dim.10.scale_ref, f32[288,384]{1,0:T(8,128)S(1)} %get-tuple-element.19.partial_ref, f32[480,128]{1,0:T(8,128)S(1)} %collective-permute-done.edge_a_ref, f32[480,128]{1,0:T(8,128)S(1)} %collective-permute-done.1.edge_b_ref), custom_call_target="tpu_custom_call" | custom-call | flops 1000000 | bytes 1400000 | tf_op jit(solution)/shard_map/corrected/pallas_call | solution.py:420
  (7 shorter events, 0.0 us)
Async XLA Ops:
  4.3 12.3 %copy-start = (s32[1536,2]{0,1:T(2,128)S(1)}, s32[1536,2]{0,1:T(2,128)}, u32[]{:S(2)}) copy-start(s32[1536,2]{0,1:T(2,128)} %param.5) | copy-start | bytes 36868
  4.3 63.9 %all-to-all-start = ((f32[32,128,128]{2,1,0:T(8,128)}), f32[32,128,128]{2,1,0:T(8,128)S(1)}, u32[]{:S(2)}, u32[]{:S(2)}) async-start(f32[32,128,128]{2,1,0:T(8,128)} %mask_pack.1), calls=%async_computation | async-start | bytes 4194304 | tf_op jit(solution)/shard_map/all_to_all | solution.py:450
  70.6 9.6 %collective-permute-start = (f32[480,128]{1,0:T(8,128)S(1)}, f32[480,128]{1,0:T(8,128)S(1)}, u32[]{:S(2)}, u32[]{:S(2)}) collective-permute-start(f32[480,128]{1,0:T(8,128)S(1)} %get-tuple-element.20), channel_id=1, source_target_pairs={{0,1},{1,2},{2,3},{3,4},{4,5},{5,6},{6,7},{7,8},{8,9},{9,10},{10,1... | collective-permute-start | bytes 737288 | tf_op jit(solution)/shard_map/ppermute | solution.py:438
  75.3 9.3 %collective-permute-start.1 = (f32[480,128]{1,0:T(8,128)S(1)}, f32[480,128]{1,0:T(8,128)S(1)}, u32[]{:S(2)}, u32[]{:S(2)}) collective-permute-start(f32[480,128]{1,0:T(8,128)S(1)} %get-tuple-element.21), channel_id=1, source_target_pairs={{1,0},{2,1},{3,2},{4,3},{5,4},{6,5},{7,6},{8,7},{9,8},{10,9},{11,1... | collective-permute-start | bytes 737288 | tf_op jit(solution)/shard_map/ppermute | solution.py:438
